TPU v7x, 32 devices: a whole 2x2x4 slice. The times are simulated.
32 devices in a mesh: rep: 2 (over x), dp: 8 (over z, y), tensor: 2 (over core).
Axes of the slice: x: 2, y: 2, z: 4, core: 2. Of those that a mesh axis runs over, the one named last changes fastest.
Arguments:
- rubric_query: bfloat16 [64, 256, 4096], P(('rep', 'dp'), None, 'tensor'), parts along dimension 0, may hold values from -48 to 48
- rubric_key: bfloat16 [64, 256, 512], P(('rep', 'dp'), None, 'tensor'), parts along dimension 0, may hold values from -4 to 4
- rubric_value: bfloat16 [64, 256, 512], P(('rep', 'dp'), None, 'tensor'), parts along dimension 0, may hold values from -6 to 6
- response_states: bfloat16 [64, 256, 8192], P(('rep', 'dp'), None, 'tensor'), parts along dimension 0, may hold values from -6 to 6
- key_weight: bfloat16 [8192, 512], P('tensor'), may hold values from -0.0625 to 0.0625
- value_weight: bfloat16 [8192, 512], P('tensor'), may hold values from -0.0625 to 0.0625
- owner_slot: int32 [64], P('rep'), parts along dimension 0, may hold values from 0 to 31, as said below
- response_length: int32 [64], P('rep'), parts along dimension 0, may hold values from 128 to 256, as said below
- pair_table: int32 [64, 2], P('rep'), parts along dimension 0, may hold values from 0 to 31, as said below
Outputs:
- judge_context: bfloat16 [64, 256, 4096], P(('rep', 'dp'), None, 'tensor'), parts along dimension 0
There are 2 independent parts, one for each index of `rep`. A program takes and returns all parts, laid end to end along the dimension named above; an argument that names none is the same for every part. Nothing has to cross between parts.
Inputs may be any that keep to these rules, and one draw needn't show every extreme that they name: A permutation: response r is stored in row owner_slot[r] of response_states, on index owner_slot[r] // 4 of dp. `response_length`: indexed by response; rows past a response's length are padding; some response has exactly 256 tokens. `pair_table`: rows 4 * g to 4 * g + 3 are the pair tasks of index g of dp; the 8 responses named in them are distinct and stored on 8 distinct indices of dp.
All inputs are finite; a program needn't handle non-finite values.
Results may differ from a plain program's by a relative error of at most 0.008.
Values may be sent and summed in bfloat16 or wider, within the bound.
No kernel may reach another device: no remote copies, remote signals or barrier semaphores. Data moves between devices by JAX's collectives and lax.ppermute only.
A program may use at most 192 MiB of HBM per device.

v0:
```python
import jax
import jax.numpy as jnp
from jax import lax
from jax.sharding import PartitionSpec as P

HEADS = 32
KVH = 4
HD = 128


def local(
    rubric_query,
    rubric_key,
    rubric_value,
    response_states,
    key_weight,
    value_weight,
    owner_slot,
    response_length,
    pair_table,
):
    group_count = lax.axis_size("dp")
    own_group = lax.axis_index("dp")
    stored_count = response_states.shape[0]
    stored_rows = response_states.shape[1]
    pair_count = rubric_query.shape[0]
    rubric_rows = rubric_query.shape[1]
    token_rows = response_states.reshape(stored_count * stored_rows, response_states.shape[2])
    part_keys = jnp.dot(token_rows, key_weight, preferred_element_type=jnp.float32)
    part_values = jnp.dot(token_rows, value_weight, preferred_element_type=jnp.float32)
    head_width = key_weight.shape[1] // lax.axis_size("tensor")
    summed_keys, summed_values = lax.psum((part_keys, part_values), "tensor")
    offset = lax.axis_index("tensor") * head_width
    summed_keys = lax.dynamic_slice_in_dim(summed_keys, offset, head_width, 1)
    summed_values = lax.dynamic_slice_in_dim(summed_values, offset, head_width, 1)
    local_keys = summed_keys.astype(jnp.bfloat16).reshape(stored_count, stored_rows, head_width)
    local_values = summed_values.astype(jnp.bfloat16).reshape(stored_count, stored_rows, head_width)
    wanted = pair_table.reshape(group_count, 2 * pair_count)
    catalog = jnp.arange(owner_slot.shape[0], dtype=jnp.int32)
    matches = wanted[:, :, None] == catalog[None, None, :]
    slot_index = jnp.sum(jnp.where(matches, owner_slot[None, None, :], 0), axis=2)
    valid_length = jnp.sum(jnp.where(matches, response_length[None, None, :], 0), axis=2)
    owner_group = slot_index // stored_count
    stored_row = slot_index % stored_count
    from_here = owner_group == own_group
    chosen_row = jnp.sum(jnp.where(from_here, stored_row, 0), axis=1)
    needed = jnp.any(from_here, axis=1)[:, None, None]
    empty_value = jnp.zeros((), jnp.bfloat16)
    outgoing_keys = jnp.where(needed, jnp.take(local_keys, chosen_row, axis=0), empty_value)
    outgoing_values = jnp.where(needed, jnp.take(local_values, chosen_row, axis=0), empty_value)
    arrived_keys, arrived_values = (
        lax.all_to_all(outgoing_keys, "dp", split_axis=0, concat_axis=0, tiled=True),
        lax.all_to_all(outgoing_values, "dp", split_axis=0, concat_axis=0, tiled=True),
    )
    source_group = lax.dynamic_index_in_dim(owner_group, own_group, 0, keepdims=False)
    pair_lengths = lax.dynamic_index_in_dim(valid_length, own_group, 0, keepdims=False)
    pair_keys = jnp.take(arrived_keys, source_group, axis=0).reshape(
        pair_count, 2 * stored_rows, head_width
    )
    pair_values = jnp.take(arrived_values, source_group, axis=0).reshape(
        pair_count, 2 * stored_rows, head_width
    )
    all_keys = jnp.concatenate([pair_keys, rubric_key], axis=1)
    all_values = jnp.concatenate([pair_values, rubric_value], axis=1)
    local_heads = head_width // HD
    group_size = HEADS // KVH
    queries = rubric_query.reshape(pair_count, rubric_rows, local_heads, group_size, HD)
    key_heads = all_keys.reshape(pair_count, -1, local_heads, HD)
    value_heads = all_values.reshape(pair_count, -1, local_heads, HD)
    scores = jnp.einsum(
        "pqkgd,plkd->pkgql", queries, key_heads, preferred_element_type=jnp.float32
    ) * HD ** (-0.5)
    positions = jnp.arange(stored_rows, dtype=jnp.int32)
    live_keys = (
        positions[None, None, :] < pair_lengths.reshape(pair_count, 2)[:, :, None]
    ).reshape(pair_count, 1, 2 * stored_rows)
    live_keys = jnp.broadcast_to(live_keys, (pair_count, rubric_rows, 2 * stored_rows))
    query_rows = jnp.arange(rubric_rows, dtype=jnp.int32)
    causal = jnp.broadcast_to(
        query_rows[:, None] >= query_rows[None, :], (pair_count, rubric_rows, rubric_rows)
    )
    allowed = jnp.concatenate([live_keys, causal], axis=2)[:, None, None]
    scores = jnp.where(allowed, scores, -1e30)
    row_peak = jnp.max(scores, axis=4, keepdims=True)
    weights_raw = jnp.where(allowed, jnp.exp(scores - row_peak), 0.0)
    denominator = jnp.sum(weights_raw, axis=4, keepdims=True)
    weights = (weights_raw / denominator).astype(jnp.bfloat16)
    context = jnp.einsum(
        "pkgql,plkd->pqkgd", weights, value_heads, preferred_element_type=jnp.float32
    )
    return context.reshape(pair_count, rubric_rows, local_heads * group_size * HD).astype(
        jnp.bfloat16
    )


def solution(mesh):
    return jax.shard_map(
        local,
        mesh=mesh,
        in_specs=(
            P(("rep", "dp"), None, "tensor"),
            P(("rep", "dp"), None, "tensor"),
            P(("rep", "dp"), None, "tensor"),
            P(("rep", "dp"), None, "tensor"),
            P("tensor", None),
            P("tensor", None),
            P("rep"),
            P("rep"),
            P("rep", None),
        ),
        out_specs=P(("rep", "dp"), None, "tensor"),
        check_vma=False,
    )
```

profile of v0, /device:TPU:0, one launch (start us, length us, event | category | flops | bytes accessed | tf_op | source)
XLA Modules:
  0.0 154.6 jit_solution(12908961891987480141)
XLA Ops:
  0.0 0.8 copy.24
  0.8 1.1 select_reduce_fusion.1
  2.2 8.3 %fusion.37 = f32[1024,512]{1,0:T(8,128)S(1)} fusion(bf16[1024,4096]{1,0:T(8,128)(2,1)} %bitcast.64, bf16[4096,512]{1,0:T(8,128)(2,1)} %param.18), kind=kOutput, calls=%fused_computation.64 | convolution fusion | flops 4294967296 | bytes 14680064 | tf_op jit(solution)/shard_map/dot_general | solution.py:30
  10.5 5.8 %fusion.38 = f32[1024,512]{1,0:T(8,128)} fusion(bf16[1024,4096]{1,0:T(8,128)(2,1)S(1)} %bitcast.65, bf16[4096,512]{1,0:T(8,128)(2,1)S(1)} %copy-done.3), kind=kOutput, calls=%fused_computation.65 | convolution fusion | flops 4294967296 | bytes 14680064 | tf_op jit(solution)/shard_map/dot_general | solution.py:29
  16.3 15.4 %all-reduce.2 = (bf16[1024,512]{1,0:T(8,128)(2,1)S(1)}, bf16[1024,512]{1,0:T(8,128)(2,1)}) all-reduce(f32[1024,512]{1,0:T(8,128)} %fusion.38, f32[1024,512]{1,0:T(8,128)S(1)} %fusion.37), channel_id=1, replica_groups=mesh['rep'=2,'dp'=8,'tensor'=2] {'tensor'}, use_global_device_ids=true, to_apply=%region_5.8 | all-reduce | flops 1048576 | bytes 6291456 | tf_op jit(solution)/shard_map/psum | solution.py:32
  31.7 1.1 dynamic-slice_convert_fusion
  32.8 0.6 gather_fusion.2
  33.5 0.6 gather_fusion
  34.1 1.3 select_select_fusion.1
  35.4 33.1 %all_to_all.10 = bf16[8,256,256]{2,1,0:T(8,128)(2,1)S(1)} all-to-all(bf16[8,256,256]{2,1,0:T(8,128)(2,1)S(1)} %get-tuple-element.17), channel_id=1, replica_groups=mesh['rep'=2,'dp'=8,'tensor'=2] {'dp'}, dimensions={0} | all-to-all | bytes 2097152 | tf_op jit(solution)/shard_map/all_to_all | solution.py:52
  68.4 3.7 %all-to-all-start = ((bf16[8,256,256]{2,1,0:T(8,128)(2,1)}), bf16[8,256,256]{2,1,0:T(8,128)(2,1)S(1)}, u32[]{:S(2)}, u32[]{:S(2)}) async-start(bf16[8,256,256]{2,1,0:T(8,128)(2,1)} %get-tuple-element.16), calls=%async_computation | async-start | bytes 2097152 | tf_op jit(solution)/shard_map/all_to_all | solution.py:53
  72.4 5.7 %copy.38 = bf16[128,8,16,128]{3,2,1,0:T(8,128)(2,1)} copy(bf16[128,8,16,128]{3,1,2,0:T(8,128)(2,1)} %bitcast.57) | data formatting | bytes 8388608
  78.3 1.0 copy.29
  79.3 2.1 %copy.25 = bf16[4,256,256]{1,2,0:T(8,128)(2,1)} copy(bf16[4,256,256]{2,1,0:T(8,128)(2,1)} %param.15) | data formatting | bytes 1048576 | tf_op args[2]
  82.0 1.2 pad_add_fusion
  83.2 0.6 gather_fusion.3
  83.8 14.2 %all-to-all-done = bf16[8,256,256]{2,1,0:T(8,128)(2,1)S(1)} async-done(((bf16[8,256,256]{2,1,0:T(8,128)(2,1)}), bf16[8,256,256]{2,1,0:T(8,128)(2,1)S(1)}, u32[]{:S(2)}, u32[]{:S(2)}) %all-to-all-start) | async-done | bytes 1048608 | tf_op jit(solution)/shard_map/all_to_all | solution.py:53
  98.0 0.6 gather_fusion.1
  98.6 1.2 broadcast_select_fusion.1
  99.9 1.3 concatenate.23
  101.7 0.8 copy.26
  102.5 26.6 %fusion.32 = (f32[4,2,8,256]{3,2,1,0:T(8,128)S(1)}, f32[4,2,8,256,768]{3,4,2,1,0:T(8,128)}) fusion(pred[4,256,768]{1,2,0:T(8,128)(4,1)} %pad_add_fusion, bf16[4,256,2,8,128]{4,3,2,1,0:T(8,128)(2,1)} %bitcast.58, bf16[4,256,2,128]{3,1,2,0:T(8,128)(2,1)} %copy.29, bf16[4,512,2,128]{3,1,2,0:T(8,128)(2,1)S(1)} %copy.28), kind=kOutput, calls=%fused_computation.63 | convolution fusion | flops 3287286528 | bytes 56950784 | tf_op jit(solution)/shard_map/sub | solution.py:85
  129.1 19.3 %fusion.15 = bf16[4,2,128,8,256]{4,2,3,1,0:T(8,128)(2,1)} fusion(f32[4,2,8,256,768]{3,4,2,1,0:T(8,128)} %get-tuple-element.21, f32[4,2,8,256]{3,2,1,0:T(8,128)S(1)} %get-tuple-element.20, bf16[4,256,2,128]{1,3,2,0:T(8,128)(2,1)S(1)} %bitcast.61, bf16[4,512,2,128]{1,3,2,0:T(8,128)(2,1)S(1)} %copy.26), kind=kOutput, calls=%fused_computation.18 | convolution fusion | flops 3251634176 | bytes 56164352 | tf_op jit(solution)/shard_map/pkgql,plkd->pqkgd/dot_general | solution.py:88
  148.4 6.2 %copy.32 = bf16[4,256,2048]{2,1,0:T(8,128)(2,1)} copy(bf16[4,256,2048]{1,2,0:T(8,128)(2,1)} %bitcast.59) | data formatting | bytes 8388608 | tf_op jit(solution)/shard_map/convert_element_type | solution.py:91
  (29 shorter events, 1.8 us)
Async XLA Ops:
  2.2 8.3 %copy-start.2 = (bf16[4,256,4096]{2,1,0:T(8,128)(2,1)S(1)}, bf16[4,256,4096]{2,1,0:T(8,128)(2,1)}, u32[]{:S(2)}) copy-start(bf16[4,256,4096]{2,1,0:T(8,128)(2,1)} %param.16) | copy-start | bytes 25165828
  2.2 8.3 %copy-start.3 = (bf16[4096,512]{1,0:T(8,128)(2,1)S(1)}, bf16[4096,512]{1,0:T(8,128)(2,1)}, u32[]{:S(2)}) copy-start(bf16[4096,512]{1,0:T(8,128)(2,1)} %param.17) | copy-start | bytes 12582916
  68.4 29.6 %all-to-all-start = ((bf16[8,256,256]{2,1,0:T(8,128)(2,1)}), bf16[8,256,256]{2,1,0:T(8,128)(2,1)S(1)}, u32[]{:S(2)}, u32[]{:S(2)}) async-start(bf16[8,256,256]{2,1,0:T(8,128)(2,1)} %get-tuple-element.16), calls=%async_computation | async-start | bytes 2097152 | tf_op jit(solution)/shard_map/all_to_all | solution.py:53
  72.4 5.7 %copy-start = (bf16[4,256,256]{2,1,0:T(8,128)(2,1)S(1)}, bf16[4,256,256]{2,1,0:T(8,128)(2,1)}, u32[]{:S(2)}) copy-start(bf16[4,256,256]{2,1,0:T(8,128)(2,1)} %param.14) | copy-start | bytes 1572868
  102.5 26.6 %copy-start.1 = (bf16[4,256,256]{1,2,0:T(8,128)(2,1)S(1)}, bf16[4,256,256]{1,2,0:T(8,128)(2,1)}, u32[]{:S(2)}) copy-start(bf16[4,256,256]{1,2,0:T(8,128)(2,1)} %copy.25) | copy-start | bytes 1572868
where the time goes:
time: 155 us
  matrix products  59.9 us (39%)
  blocking collectives  48.5 us (31%)
  local copies, waits for them, and re-layouts  22.8 us (15%)
  waiting for transfers between devices  14.2 us (9%)
  other arithmetic  5.1 us (3%)
  starting transfers between devices  3.74 us (2%)
    all_to_all x1, blocking collectives, local(): lax.all_to_all(outgoing_keys, 'dp', split_axis=0, concat_axis=0, tiled=True)  33.1 us
    sub x1, matrix products, local(): weights_raw = jnp.where(allowed, jnp.exp(scores - row_peak), 0.0)  26.6 us
    dot_general x1, matrix products, local(): jnp.einsum('pkgql,plkd->pqkgd', weights, value_heads, preferred_element_t...  19.3 us
    psum x1, blocking collectives, local(): summed_keys, summed_values = lax.psum((part_keys, part_values), 'tensor')  15.4 us
    all_to_all x1, waiting for transfers between devices, local(): lax.all_to_all(outgoing_values, 'dp', split_axis=0, concat_axis=0, tiled=...  14.2 us
    unnamed x16, local copies, waits for them, and re-layouts  8.82 us
    dot_general x1, matrix products, local(): jnp.dot(token_rows, value_weight, preferred_element_type=jnp.float32)  8.28 us
    convert_element_type x1, local copies, waits for them, and re-layouts, local(): context.reshape(pair_count, rubric_rows, local_heads * group_size * HD)  6.19 us
  transfers between devices with their start and end apart: 1, of which 1 were waited for; matrix products, arithmetic and copies ran while one was open for 7% of the time, Pallas kernels for 0%

commit v1 on v0

v1 whole, which is shorter than its diff:
```python
import functools
import math

import jax
import jax.numpy as jnp
from jax import lax
from jax.experimental import pallas as pl
from jax.experimental.pallas import tpu as pltpu
from jax.sharding import PartitionSpec as P

HD = 128
SCALE = HD ** (-0.5) * math.log2(math.e)
VMEM_LIMIT = 48 * 1024 * 1024
FIELDS = 4
HEADS_STEP = 4
SUM_ROWS = 16
IN_FLIGHT = 5
HINT = 1
ANY = pl.BlockSpec(memory_space=pl.ANY)


def params(*semantics):
    return pltpu.CompilerParams(
        dimension_semantics=semantics or None, vmem_limit_bytes=VMEM_LIMIT
    )


def hint(flops, bytes_accessed, transcendentals):
    return pl.CostEstimate(
        flops=flops // HINT,
        bytes_accessed=bytes_accessed // HINT,
        transcendentals=transcendentals // HINT,
    )


def plan_kernel(groups, stored, slots, me_ref, owner_ref, length_ref, table_ref, plan_ref):
    me = me_ref[0]

    def one(shift, carry):
        partner = lax.bitwise_xor(me, shift)
        send_row = jnp.int32(0)
        pair = jnp.int32(0)
        length = jnp.int32(0)
        wanted = jnp.int32(0)
        for j in range(slots):
            theirs = table_ref[partner * (slots // 2) + j // 2, j % 2]
            slot = owner_ref[theirs]
            send_row = jnp.where(lax.div(slot, stored) == me, lax.rem(slot, stored), send_row)
            ours = table_ref[me * (slots // 2) + j // 2, j % 2]
            hit = lax.div(owner_ref[ours], stored) == partner
            pair = jnp.where(hit, j // 2, pair)
            length = jnp.where(hit, length_ref[ours], length)
            wanted = jnp.where(hit, 1, wanted)
        plan_ref[shift * FIELDS] = send_row
        plan_ref[shift * FIELDS + 1] = pair
        plan_ref[shift * FIELDS + 2] = length
        plan_ref[shift * FIELDS + 3] = wanted
        return carry

    lax.fori_loop(0, groups, one, 0)


def make_plan(me, owner_slot, response_length, pair_table, groups, stored, pairs):
    smem = pl.BlockSpec(memory_space=pltpu.SMEM)
    return pl.pallas_call(
        functools.partial(plan_kernel, groups, stored, 2 * pairs),
        out_shape=jax.ShapeDtypeStruct((groups * FIELDS,), jnp.int32),
        in_specs=[smem] * 4,
        out_specs=smem,
        name="plan",
    )(me, owner_slot, response_length, pair_table)


def project_kernel(half_ref, x_ref, key_ref, value_ref, *refs):
    out_ref = refs[-1]
    width = key_ref.shape[1]
    x = x_ref[...]
    for at, weight_ref in enumerate((key_ref, value_ref)):
        columns = slice(at * width, (at + 1) * width)
        part = jnp.dot(x, weight_ref[...], preferred_element_type=jnp.float32)

        @pl.when(pl.program_id(0) == 0)
        def _():
            out_ref[:, columns] = part

        @pl.when(pl.program_id(0) > 0)
        def _():
            out_ref[:, columns] += part


def project(rows, key_weight, value_weight, half, width, name, after=()):
    total, depth = rows.shape
    chunk = 512
    weight_spec = pl.BlockSpec((chunk, width), lambda k, half: (k, half[0]))
    return pl.pallas_call(
        project_kernel,
        grid_spec=pltpu.PrefetchScalarGridSpec(
            num_scalar_prefetch=1,
            grid=(depth // chunk,),
            in_specs=[pl.BlockSpec((total, chunk), lambda k, half: (0, k)), weight_spec, weight_spec]
            + [ANY] * len(after),
            out_specs=pl.BlockSpec((total, 2 * width), lambda k, half: (0, 0)),
        ),
        out_shape=jax.ShapeDtypeStruct((total, 2 * width), jnp.float32),
        compiler_params=params("arbitrary"),
        cost_estimate=hint(
            4 * total * depth * width, 2 * total * depth + 4 * depth * width + 8 * total * width, 0
        ),
        name=name,
    )(half, rows, key_weight, value_weight, *after)


def finish_kernel(length, width, plan_ref, own_ref, other_ref, *out_refs):
    for shift, out_ref in enumerate(out_refs):
        start = pl.multiple_of(plan_ref[shift * FIELDS] * length, length)
        rows = pl.ds(start, length)
        for at in range(2):
            columns = slice(at * width, (at + 1) * width)
            total = own_ref[rows, columns] + other_ref[rows, columns]
            out_ref[at * length : (at + 1) * length, :] = total.astype(out_ref.dtype)


def finish(plan, own, other, groups, length, name):
    width = own.shape[1] // 2
    vmem = pl.BlockSpec(memory_space=pltpu.VMEM)
    return pl.pallas_call(
        functools.partial(finish_kernel, length, width),
        out_shape=[jax.ShapeDtypeStruct((2 * length, width), jnp.bfloat16)] * groups,
        in_specs=[pl.BlockSpec(memory_space=pltpu.SMEM), vmem, vmem],
        out_specs=[vmem] * groups,
        compiler_params=params(),
        cost_estimate=hint(
            2 * groups * length * width,
            16 * own.shape[0] * width + 4 * groups * length * width,
            0,
        ),
        name=name,
    )(plan, own, other)


def scores_of(keys, queries):
    return lax.dot_general(
        keys, queries, (((1,), (1,)), ((), ())), preferred_element_type=jnp.float32
    )


def rubric_kernel(q_ref, k_ref, v_ref, *refs):
    acc_ref, ml_ref = refs[-2:]
    keys = k_ref[0]
    count = keys.shape[0]
    values = jnp.concatenate(
        [v_ref[0].T, jnp.ones((SUM_ROWS, count), jnp.bfloat16)], axis=0
    )
    shape = (count, q_ref.shape[1])
    causal = lax.broadcasted_iota(jnp.int32, shape, 0) <= lax.broadcasted_iota(jnp.int32, shape, 1)
    for h in range(HEADS_STEP):
        s = scores_of(keys, q_ref[0, :, h * HD : (h + 1) * HD])
        s = jnp.where(causal, s, -1e30)
        peak = jnp.max(s, axis=0, keepdims=True)
        weights = jnp.exp2((s - peak) * SCALE).astype(jnp.bfloat16)
        pv = jnp.dot(values, weights, preferred_element_type=jnp.float32)
        acc_ref[0, h * HD : (h + 1) * HD, :] = pv[:HD]
        ml_ref[0, 0, h : h + 1, :] = peak
        ml_ref[0, 0, HEADS_STEP + h : HEADS_STEP + h + 1, :] = pv[HD : HD + 1]


def rubric_attention(first, some, query, key, value, state, after=()):
    pairs, rows, width = query.shape
    heads = width // HD
    steps = heads // HEADS_STEP
    per_head = steps * HD // key.shape[2]
    step_width = HEADS_STEP * HD
    count = key.shape[1]
    return pl.pallas_call(
        rubric_kernel,
        grid=(some, steps),
        in_specs=[
            pl.BlockSpec((1, rows, step_width), lambda p, g: (first + p, 0, g)),
            pl.BlockSpec((1, count, HD), lambda p, g: (first + p, 0, g // per_head)),
            pl.BlockSpec((1, count, HD), lambda p, g: (first + p, 0, g // per_head)),
        ]
        + [ANY] * (len(state) + len(after)),
        out_specs=[
            pl.BlockSpec((1, step_width, rows), lambda p, g: (first + p, g, 0)),
            pl.BlockSpec((1, 1, 2 * HEADS_STEP, rows), lambda p, g: (first + p, g, 0, 0)),
        ],
        out_shape=[
            jax.ShapeDtypeStruct((pairs, width, rows), jnp.float32),
            jax.ShapeDtypeStruct((pairs, steps, 2 * HEADS_STEP, rows), jnp.float32),
        ],
        input_output_aliases={3: 0, 4: 1} if state else {},
        compiler_params=params("arbitrary", "arbitrary"),
        cost_estimate=hint(4 * some * heads * rows * count * HD, some * rows * width * 6, some * heads * rows * count),
        name="rubric_attention",
    )(query, key, value, *state, *after)


def response_kernel(shift, per_head, plan_ref, q_ref, kv_ref, acc_ref, ml_ref, *refs):
    acc_out, ml_out, out_ref, keys_ref, values_ref = refs[-5:]
    count = kv_ref.shape[0] // 2
    kv_heads = kv_ref.shape[1] // HD
    length = plan_ref[shift * FIELDS + 2]
    wanted = plan_ref[shift * FIELDS + 3] == 1
    step = pl.program_id(0)

    @pl.when(step == 0)
    def _():
        live_rows = lax.broadcasted_iota(jnp.int32, (count, HD), 0) < length
        live_columns = lax.broadcasted_iota(jnp.int32, (HD + SUM_ROWS, count), 1) < length
        for kv in range(kv_heads):
            columns = slice(kv * HD, (kv + 1) * HD)
            block = kv_ref[:count, columns].astype(jnp.float32)
            keys_ref[kv] = jnp.where(live_rows, block, block[0:1]).astype(jnp.bfloat16)
            block = kv_ref[count:, columns].astype(jnp.float32)
            values = jnp.concatenate(
                [block.T, jnp.ones((SUM_ROWS, count), jnp.float32)], axis=0
            )
            values_ref[kv] = jnp.where(live_columns, values, 0.0).astype(jnp.bfloat16)

    def emit(h, acc, total):
        out_ref[0, :, h * HD : (h + 1) * HD] = (acc * (1.0 / total)).T.astype(out_ref.dtype)

    @pl.when(wanted)
    def _():
        keys = keys_ref[step // per_head]
        values = values_ref[step // per_head]
        for h in range(HEADS_STEP):
            head = slice(h * HD, (h + 1) * HD)
            peak_row = slice(h, h + 1)
            total_row = slice(HEADS_STEP + h, HEADS_STEP + h + 1)
            s = scores_of(keys, q_ref[0, :, head])
            old_peak = ml_ref[0, 0, peak_row, :]
            peak = jnp.maximum(old_peak, jnp.max(s, axis=0, keepdims=True))
            weights = jnp.exp2((s - peak) * SCALE).astype(jnp.bfloat16)
            fade = jnp.exp2((old_peak - peak) * SCALE)
            pv = jnp.dot(values, weights, preferred_element_type=jnp.float32)
            acc = acc_ref[0, head, :] * fade + pv[:HD]
            total = ml_ref[0, 0, total_row, :] * fade + pv[HD : HD + 1]
            acc_out[0, head, :] = acc
            ml_out[0, 0, peak_row, :] = peak
            ml_out[0, 0, total_row, :] = total
            emit(h, acc, total)

    @pl.when(jnp.logical_not(wanted))
    def _():
        acc_out[...] = acc_ref[...]
        ml_out[...] = ml_ref[...]
        for h in range(HEADS_STEP):
            emit(
                h,
                acc_ref[0, h * HD : (h + 1) * HD, :],
                ml_ref[0, 0, HEADS_STEP + h : HEADS_STEP + h + 1, :],
            )


def response_attention(shift, plan, query, kv, acc, ml, out):
    pairs, rows, width = query.shape
    heads = width // HD
    steps = heads // HEADS_STEP
    per_head = steps * HD // kv.shape[1]
    step_width = HEADS_STEP * HD
    count = kv.shape[0] // 2
    pair_at = shift * FIELDS + 1
    acc_spec = pl.BlockSpec((1, step_width, rows), lambda g, plan: (plan[pair_at], g, 0))
    ml_spec = pl.BlockSpec((1, 1, 2 * HEADS_STEP, rows), lambda g, plan: (plan[pair_at], g, 0, 0))
    row_spec = pl.BlockSpec((1, rows, step_width), lambda g, plan: (plan[pair_at], 0, g))
    operands = [plan, query, kv, acc, ml]
    in_specs = [row_spec, pl.BlockSpec(kv.shape, lambda g, plan: (0, 0)), acc_spec, ml_spec]
    aliases = {3: 0, 4: 1}
    if out is not None:
        operands.append(out)
        in_specs.append(pl.BlockSpec(memory_space=pl.ANY))
        aliases[5] = 2
    return pl.pallas_call(
        functools.partial(response_kernel, shift, per_head),
        grid_spec=pltpu.PrefetchScalarGridSpec(
            num_scalar_prefetch=1,
            grid=(steps,),
            in_specs=in_specs,
            out_specs=[acc_spec, ml_spec, row_spec],
            scratch_shapes=[
                pltpu.VMEM((kv.shape[1] // HD, count, HD), jnp.bfloat16),
                pltpu.VMEM((kv.shape[1] // HD, HD + SUM_ROWS, count), jnp.bfloat16),
            ],
        ),
        out_shape=[
            jax.ShapeDtypeStruct(acc.shape, acc.dtype),
            jax.ShapeDtypeStruct(ml.shape, ml.dtype),
            jax.ShapeDtypeStruct(query.shape, jnp.bfloat16),
        ],
        input_output_aliases=aliases,
        compiler_params=params("arbitrary"),
        cost_estimate=hint(4 * heads * rows * count * HD, rows * width * 12, heads * rows * count),
        name="response_attention",
    )(*operands)


def local(
    rubric_query,
    rubric_key,
    rubric_value,
    response_states,
    key_weight,
    value_weight,
    owner_slot,
    response_length,
    pair_table,
):
    groups = lax.axis_size("dp")
    stored, length, depth = response_states.shape
    pairs = rubric_query.shape[0]
    tensor = lax.axis_size("tensor")
    width = key_weight.shape[1] // tensor
    me = lax.axis_index("dp").astype(jnp.int32)
    own_half = lax.axis_index("tensor").astype(jnp.int32)
    other_half = 1 - own_half
    rows = response_states.reshape(stored * length, depth)
    swap = [(0, 1), (1, 0)]
    plan = make_plan(
        me[None], owner_slot, response_length, pair_table, groups, stored, pairs
    )

    other = project(rows, key_weight, value_weight, other_half[None], width, "other_half")
    received = lax.ppermute(other, "tensor", swap)
    own = project(rows, key_weight, value_weight, own_half[None], width, "own_half", after=[other])
    blocks = finish(plan, own, received, groups, length, "finish")

    far = list(range(groups - 1, groups // 2 - 1, -1))
    near = list(range(groups // 2 - 1, 0, -1))
    order = []
    for at in range(len(far)):
        order += far[at : at + 1] + near[at : at + 1]
    arrived = {}

    def send(shift, *after):
        block = lax.optimization_barrier((blocks[shift], *after))[0]
        arrived[shift] = lax.ppermute(block, "dp", [(g, g ^ shift) for g in range(groups)])

    for shift in order[:IN_FLIGHT]:
        send(shift)
    state = rubric_attention(
        0, pairs, rubric_query, rubric_key, rubric_value, (), after=[blocks[0]]
    )
    acc, ml, out = response_attention(0, plan, rubric_query, blocks[0], *state, None)
    for at, shift in enumerate(order):
        if at + IN_FLIGHT < len(order):
            send(order[at + IN_FLIGHT], arrived[shift], ml)
        acc, ml, out = response_attention(shift, plan, rubric_query, arrived[shift], acc, ml, out)
    return out


def solution(mesh):
    return jax.shard_map(
        local,
        mesh=mesh,
        in_specs=(
            P(("rep", "dp"), None, "tensor"),
            P(("rep", "dp"), None, "tensor"),
            P(("rep", "dp"), None, "tensor"),
            P(("rep", "dp"), None, "tensor"),
            P("tensor", None),
            P("tensor", None),
            P("rep"),
            P("rep"),
            P("rep", None),
        ),
        out_specs=P(("rep", "dp"), None, "tensor"),
        check_vma=False,
    )
```

time: 155 us -> 135 us (0.87)
  Pallas kernels: 0 us -> 121 us
  matrix products: 59.9 us -> 0 us
  blocking collectives: 48.5 us -> 0 us
  local copies, waits for them, and re-layouts: 22.8 us -> 0.72 us
  waiting for transfers between devices: 14.2 us -> 0.02 us
  starting transfers between devices: 3.74 us -> 12.5 us
  other arithmetic: 5.1 us -> 0 us
    pallas_call x0 -> x13, Pallas kernels: none -> 121 us  [the longest x8 66.5 us: response_attention(): pl.pallas_call(functools.partial(response_kernel, shift, per_head), grid_...]
    dot_general x3 -> x0, matrix products: 33.4 us -> none  [the longest x1 19.3 us: local(): jnp.einsum('pkgql,plkd->pqkgd', weights, value_heads, preferred_element_t...]
    all_to_all x1 -> x0, blocking collectives: 33.1 us -> none  [local(): lax.all_to_all(outgoing_keys, 'dp', split_axis=0, concat_axis=0, tiled=True)]
    sub x1 -> x0, matrix products: 26.6 us -> none  [local(): weights_raw = jnp.where(allowed, jnp.exp(scores - row_peak), 0.0)]
    psum x1 -> x0, blocking collectives: 15.4 us -> none  [local(): summed_keys, summed_values = lax.psum((part_keys, part_values), 'tensor')]
    all_to_all x1 -> x0, waiting for transfers between devices: 14.2 us -> none  [local(): lax.all_to_all(outgoing_values, 'dp', split_axis=0, concat_axis=0, tiled=...]
    ppermute x0 -> x8, starting transfers between devices: none -> 12.5 us  [the longest x7 12 us: send(): lax.ppermute(block, 'dp', [(g, g ^ shift) for g in range(groups)])]
    unnamed x16 -> x11, local copies, waits for them, and re-layouts: 8.82 us -> 0.72 us
  transfers between devices with their start and end apart: 1 -> 8, of which waited for: 1 -> 0; matrix products, arithmetic and copies ran while one was open for 7% -> 1% of each run, Pallas kernels for 0% -> 72%
where the time goes in v1:
time: 135 us
  Pallas kernels  121 us (90%)
  starting transfers between devices  12.5 us (9%)
    pallas_call x8, Pallas kernels, response_attention(): pl.pallas_call(functools.partial(response_kernel, shift, per_head), grid_...  66.5 us
    pallas_call x2, Pallas kernels, project(): pl.pallas_call(project_kernel, grid_spec=pltpu.PrefetchScalarGridSpec(num...  28.7 us
    pallas_call x1, Pallas kernels, rubric_attention(): pl.pallas_call(rubric_kernel, grid=(some, steps), in_specs=[pl.BlockSpec(...  21.8 us
    ppermute x7, starting transfers between devices, send(): lax.ppermute(block, 'dp', [(g, g ^ shift) for g in range(groups)])  12 us
  transfers between devices with their start and end apart: 8, of which 0 were waited for; matrix products, arithmetic and copies ran while one was open for 1% of the time, Pallas kernels for 72%

profile of v1, /device:TPU:0, one launch (start us, length us, event | category | flops | bytes accessed | tf_op | source)
XLA Modules:
  0.0 134.6 jit_solution(10541728566706282319)
XLA Ops:
  0.0 14.3 %other_half.1.refs_0_ = f32[1024,512]{1,0:T(8,128)S(1)} custom-call(s32[1]{0:T(128)} %bitcast.3.half_ref, bf16[1024,4096]{1,0:T(8,128)(2,1)} %bitcast.4, bf16[4096,512]{1,0:T(8,128)(2,1)} %key_ref.3, bf16[4096,512]{1,0:T(8,128)(2,1)} %value_ref.3), custom_call_target="tpu_custom_call" | custom-call | flops 4294967296 | bytes 14680064 | tf_op jit(solution)/shard_map/other_half/pallas_call | solution.py:95
  14.3 0.5 collective-permute-start
  14.8 0.7 copy.33.table_ref
  15.5 2.0 %plan.1.plan_ref = s32[32]{0:T(128)} custom-call(s32[1]{0:T(128)} %bitcast.me_ref, s32[32]{0:T(128)} %owner_ref.1, s32[32]{0:T(128)} %length_ref.1, s32[32,2]{1,0:T(8,128)} %copy.33.table_ref), custom_call_target="tpu_custom_call" | custom-call | tf_op jit(solution)/shard_map/plan/pallas_call | solution.py:65
  17.5 0.0 copy-start.2
  17.5 0.0 copy-start.3
  17.6 14.4 %own_half.1.own_ref = f32[1024,512]{1,0:T(8,128)S(1)} custom-call(s32[1]{0:T(128)} %bitcast.1.half_ref, bf16[1024,4096]{1,0:T(8,128)(2,1)} %bitcast.5, bf16[4096,512]{1,0:T(8,128)(2,1)} %key_ref.3, bf16[4096,512]{1,0:T(8,128)(2,1)} %value_ref.3, f32[1024,512]{1,0:T(8,128)S(1)} %other_half.1.refs_0_), custom_call_target="tpu_custom_call" | custom-call | flops 4294967296 | bytes 14680064 | tf_op jit(solution)/shard_map/own_half/pallas_call | solution.py:95
  31.9 0.0 copy-start
  32.0 2.2 %finish.1 = (bf16[512,256]{1,0:T(8,128)(2,1)S(1)}, bf16[512,256]{1,0:T(8,128)(2,1)S(1)}, bf16[512,256]{1,0:T(8,128)(2,1)S(1)}, bf16[512,256]{1,0:T(8,128)(2,1)S(...) custom-call(s32[32]{0:T(128)S(1)} %copy-done.1, ...), custom_call_target="tpu_custom_call" | custom-call | flops 1048576 | bytes 6291456 | tf_op jit(solution)/shard_map/finish/pallas_call | solution.py:126
  34.2 5.6 %collective-permute-start.2 = (bf16[512,256]{1,0:T(8,128)(2,1)S(1)}, bf16[512,256]{1,0:T(8,128)(2,1)S(1)}, u32[]{:S(2)}, u32[]{:S(2)}) collective-permute-start(bf16[512,256]{1,0:T(8,128)(2,1)S(1)} %get-tuple-element.41), channel_id=1, source_target_pairs={{0,14},{2,12},{4,10},{6,8},{8,6},{10,4},{12,2},{14,0},{1,15},{3,13... | collective-permute-start | bytes 786440 | tf_op jit(solution)/shard_map/ppermute | solution.py:337
  39.9 1.7 %collective-permute-start.5 = (bf16[512,256]{1,0:T(8,128)(2,1)S(1)}, bf16[512,256]{1,0:T(8,128)(2,1)S(1)}, u32[]{:S(2)}, u32[]{:S(2)}) collective-permute-start(bf16[512,256]{1,0:T(8,128)(2,1)S(1)} %get-tuple-element.52), channel_id=1, source_target_pairs={{0,10},{2,8},{4,14},{6,12},{8,2},{10,0},{12,6},{14,4},{1,11},{3,9}... | collective-permute-start | bytes 786440 | tf_op jit(solution)/shard_map/ppermute | solution.py:337
  41.5 0.7 collective-permute-start.6
  42.2 2.9 %collective-permute-start.7 = (bf16[512,256]{1,0:T(8,128)(2,1)S(1)}, bf16[512,256]{1,0:T(8,128)(2,1)S(1)}, u32[]{:S(2)}, u32[]{:S(2)}) collective-permute-start(bf16[512,256]{1,0:T(8,128)(2,1)S(1)} %get-tuple-element.54), channel_id=1, source_target_pairs={{0,12},{2,14},{4,8},{6,10},{8,4},{10,6},{12,0},{14,2},{1,13},{3,15... | collective-permute-start | bytes 786440 | tf_op jit(solution)/shard_map/ppermute | solution.py:337
  45.2 21.8 %rubric_attention.1 = (f32[4,2048,256]{2,1,0:T(8,128)}, f32[4,4,8,256]{3,2,1,0:T(8,128)S(1)}) custom-call(bf16[4,256,2048]{2,1,0:T(8,128)(2,1)S(1)} %copy-done, bf16[4,256,256]{2,1,0:T(8,128)(2,1)S(1)} %copy-done.2, bf16[4,256,256]{2,1,0:T(8,128)(2,1)S(1)} %copy-done.3, bf16[512,256]{1,0:T(8,128)(2,1)S(1)} %get-tuple-element.42.refs_0_.kv_ref), custom_call_target="tpu_custom_call" | custom-call | flops 2147483648 | bytes 12582912 | tf_op jit(solution)/shard_map/rubric_attention/pallas_call | solution.py:174
  67.0 8.3 %response_attention.8 = (f32[4,2048,256]{2,1,0:T(8,128)}, f32[4,4,8,256]{3,2,1,0:T(8,128)S(1)}, bf16[4,256,2048]{2,1,0:T(8,128)(2,1)}) custom-call(s32[32]{0:T(128)S(1)} %copy-done.1, bf16[4,256,2048]{2,1,0:T(8,128)(2,1)S(1)} %copy-done, bf16[512,256]{1,0:T(8,128)(2,1)S(1)} %get-tuple-element.42.refs_0_.kv_ref, ...), custom_call_target="tpu_custom_call", output_to_operand_aliasing={{0}: (3, {}), {1}: (4, {})} | custom-call | flops 536870912 | bytes 6291456 | tf_op jit(solution)/shard_map/response_attention/pallas_call | solution.py:274
  75.3 0.6 collective-permute-start.4
  75.8 8.3 %response_attention.9 = (f32[4,2048,256]{2,1,0:T(8,128)}, f32[4,4,8,256]{3,2,1,0:T(8,128)S(1)}, bf16[4,256,2048]{2,1,0:T(8,128)(2,1)}) custom-call(s32[32]{0:T(128)S(1)} %copy-done.1, bf16[4,256,2048]{2,1,0:T(8,128)(2,1)S(1)} %copy-done, ...), custom_call_target="tpu_custom_call", output_to_operand_aliasing={{0}: (3, {}), {1}: (4, {}), {2}: (5, {})} | custom-call | flops 536870912 | bytes 6291456 | tf_op jit(solution)/shard_map/response_attention/pallas_call | solution.py:274
  84.1 0.5 collective-permute-start.3
  84.7 8.3 %response_attention.10 = (f32[4,2048,256]{2,1,0:T(8,128)}, f32[4,4,8,256]{3,2,1,0:T(8,128)S(1)}, bf16[4,256,2048]{2,1,0:T(8,128)(2,1)}) custom-call(s32[32]{0:T(128)S(1)} %copy-done.1, bf16[4,256,2048]{2,1,0:T(8,128)(2,1)S(1)} %copy-done, ...), custom_call_target="tpu_custom_call", output_to_operand_aliasing={{0}: (3, {}), {1}: (4, {}), {2}: (5, {})} | custom-call | flops 536870912 | bytes 6291456 | tf_op jit(solution)/shard_map/response_attention/pallas_call | solution.py:274
  93.0 8.3 %response_attention.11 = (f32[4,2048,256]{2,1,0:T(8,128)}, f32[4,4,8,256]{3,2,1,0:T(8,128)S(1)}, bf16[4,256,2048]{2,1,0:T(8,128)(2,1)}) custom-call(s32[32]{0:T(128)S(1)} %copy-done.1, bf16[4,256,2048]{2,1,0:T(8,128)(2,1)S(1)} %copy-done, ...), custom_call_target="tpu_custom_call", output_to_operand_aliasing={{0}: (3, {}), {1}: (4, {}), {2}: (5, {})} | custom-call | flops 536870912 | bytes 6291456 | tf_op jit(solution)/shard_map/response_attention/pallas_call | solution.py:274
  101.3 8.3 %response_attention.12 = (f32[4,2048,256]{2,1,0:T(8,128)}, f32[4,4,8,256]{3,2,1,0:T(8,128)S(1)}, bf16[4,256,2048]{2,1,0:T(8,128)(2,1)}) custom-call(s32[32]{0:T(128)S(1)} %copy-done.1, bf16[4,256,2048]{2,1,0:T(8,128)(2,1)S(1)} %copy-done, ...), custom_call_target="tpu_custom_call", output_to_operand_aliasing={{0}: (3, {}), {1}: (4, {}), {2}: (5, {})} | custom-call | flops 536870912 | bytes 6291456 | tf_op jit(solution)/shard_map/response_attention/pallas_call | solution.py:274
  109.6 8.3 %response_attention.13 = (f32[4,2048,256]{2,1,0:T(8,128)}, f32[4,4,8,256]{3,2,1,0:T(8,128)S(1)}, bf16[4,256,2048]{2,1,0:T(8,128)(2,1)}) custom-call(s32[32]{0:T(128)S(1)} %copy-done.1, bf16[4,256,2048]{2,1,0:T(8,128)(2,1)S(1)} %copy-done, ...), custom_call_target="tpu_custom_call", output_to_operand_aliasing={{0}: (3, {}), {1}: (4, {}), {2}: (5, {})} | custom-call | flops 536870912 | bytes 6291456 | tf_op jit(solution)/shard_map/response_attention/pallas_call | solution.py:274
  117.9 8.3 %response_attention.14 = (f32[4,2048,256]{2,1,0:T(8,128)}, f32[4,4,8,256]{3,2,1,0:T(8,128)S(1)}, bf16[4,256,2048]{2,1,0:T(8,128)(2,1)}) custom-call(s32[32]{0:T(128)S(1)} %copy-done.1, bf16[4,256,2048]{2,1,0:T(8,128)(2,1)S(1)} %copy-done, ...), custom_call_target="tpu_custom_call", output_to_operand_aliasing={{0}: (3, {}), {1}: (4, {}), {2}: (5, {})} | custom-call | flops 536870912 | bytes 6291456 | tf_op jit(solution)/shard_map/response_attention/pallas_call | solution.py:274
  126.3 8.3 %response_attention.15 = (f32[4,2048,256]{2,1,0:T(8,128)}, f32[4,4,8,256]{3,2,1,0:T(8,128)S(1)}, bf16[4,256,2048]{2,1,0:T(8,128)(2,1)}) custom-call(s32[32]{0:T(128)S(1)} %copy-done.1, bf16[4,256,2048]{2,1,0:T(8,128)(2,1)S(1)} %copy-done, ...), custom_call_target="tpu_custom_call", output_to_operand_aliasing={{0}: (3, {}), {1}: (4, {}), {2}: (5, {})} | custom-call | flops 536870912 | bytes 6291456 | tf_op jit(solution)/shard_map/response_attention/pallas_call | solution.py:274
  (16 shorter events, 0.0 us)
Async XLA Ops:
  0.0 14.8 %copy-start.4 = (s32[32,2]{0,1:T(2,128)S(1)}, s32[32,2]{0,1:T(2,128)}, u32[]{:S(2)}) copy-start(s32[32,2]{0,1:T(2,128)} %param.17) | copy-start | bytes 772
  14.3 17.7 %collective-permute-start = (f32[1024,512]{1,0:T(8,128)S(1)}, f32[1024,512]{1,0:T(8,128)}, u32[]{:S(2)}, u32[]{:S(2)}) collective-permute-start(f32[1024,512]{1,0:T(8,128)S(1)} %other_half.1.refs_0_), channel_id=1, source_target_pairs={{0,1},{1,0},{2,3},{3,2},{4,5},{5,4},{6,7},{7,6},{8,9},{9,8},{10,11... | collective-permute-start | bytes 6291464 | tf_op jit(solution)/shard_map/ppermute | solution.py:324
  17.5 14.4 %copy-start.1 = (s32[32]{0:T(128)S(1)}, s32[32]{0:T(128)}, u32[]{:S(2)}) copy-start(s32[32]{0:T(128)} %plan.1.plan_ref) | copy-start | bytes 388
  17.5 27.6 %copy-start.2 = (bf16[4,256,256]{2,1,0:T(8,128)(2,1)S(1)}, bf16[4,256,256]{2,1,0:T(8,128)(2,1)}, u32[]{:S(2)}) copy-start(bf16[4,256,256]{2,1,0:T(8,128)(2,1)} %k_ref.1) | copy-start | bytes 1572868
  17.5 27.6 %copy-start.3 = (bf16[4,256,256]{2,1,0:T(8,128)(2,1)S(1)}, bf16[4,256,256]{2,1,0:T(8,128)(2,1)}, u32[]{:S(2)}) copy-start(bf16[4,256,256]{2,1,0:T(8,128)(2,1)} %v_ref.1) | copy-start | bytes 1572868
  31.9 13.2 %copy-start = (bf16[4,256,2048]{2,1,0:T(8,128)(2,1)S(1)}, bf16[4,256,2048]{2,1,0:T(8,128)(2,1)}, u32[]{:S(2)}) copy-start(bf16[4,256,2048]{2,1,0:T(8,128)(2,1)} %q_ref.17) | copy-start | bytes 12582916
  34.2 41.1 %collective-permute-start.2 = (bf16[512,256]{1,0:T(8,128)(2,1)S(1)}, bf16[512,256]{1,0:T(8,128)(2,1)S(1)}, u32[]{:S(2)}, u32[]{:S(2)}) collective-permute-start(bf16[512,256]{1,0:T(8,128)(2,1)S(1)} %get-tuple-element.41), channel_id=1, source_target_pairs={{0,14},{2,12},{4,10},{6,8},{8,6},{10,4},{12,2},{14,0},{1,15},{3,13... | collective-permute-start | bytes 786440 | tf_op jit(solution)/shard_map/ppermute | solution.py:337
  39.9 44.3 %collective-permute-start.1 = (bf16[512,256]{1,0:T(8,128)(2,1)S(1)}, bf16[512,256]{1,0:T(8,128)(2,1)S(1)}, u32[]{:S(2)}, u32[]{:S(2)}) collective-permute-start(bf16[512,256]{1,0:T(8,128)(2,1)S(1)} %get-tuple-element.40), channel_id=1, source_target_pairs={{0,6},{2,4},{4,2},{6,0},{8,14},{10,12},{12,10},{14,8},{1,7},{3,5},... | collective-permute-start | bytes 786440 | tf_op jit(solution)/shard_map/ppermute | solution.py:337
  39.9 69.8 %collective-permute-start.5 = (bf16[512,256]{1,0:T(8,128)(2,1)S(1)}, bf16[512,256]{1,0:T(8,128)(2,1)S(1)}, u32[]{:S(2)}, u32[]{:S(2)}) collective-permute-start(bf16[512,256]{1,0:T(8,128)(2,1)S(1)} %get-tuple-element.52), channel_id=1, source_target_pairs={{0,10},{2,8},{4,14},{6,12},{8,2},{10,0},{12,6},{14,4},{1,11},{3,9}... | collective-permute-start | bytes 786440 | tf_op jit(solution)/shard_map/ppermute | solution.py:337
  41.5 59.8 %collective-permute-start.6 = (bf16[512,256]{1,0:T(8,128)(2,1)S(1)}, bf16[512,256]{1,0:T(8,128)(2,1)S(1)}, u32[]{:S(2)}, u32[]{:S(2)}) collective-permute-start(bf16[512,256]{1,0:T(8,128)(2,1)S(1)} %get-tuple-element.53), channel_id=1, source_target_pairs={{0,4},{2,6},{4,0},{6,2},{8,12},{10,14},{12,8},{14,10},{1,5},{3,7},... | collective-permute-start | bytes 786440 | tf_op jit(solution)/shard_map/ppermute | solution.py:337
  42.2 50.8 %collective-permute-start.7 = (bf16[512,256]{1,0:T(8,128)(2,1)S(1)}, bf16[512,256]{1,0:T(8,128)(2,1)S(1)}, u32[]{:S(2)}, u32[]{:S(2)}) collective-permute-start(bf16[512,256]{1,0:T(8,128)(2,1)S(1)} %get-tuple-element.54), channel_id=1, source_target_pairs={{0,12},{2,14},{4,8},{6,10},{8,4},{10,6},{12,0},{14,2},{1,13},{3,15... | collective-permute-start | bytes 786440 | tf_op jit(solution)/shard_map/ppermute | solution.py:337
  75.3 42.7 %collective-permute-start.4 = (bf16[512,256]{1,0:T(8,128)(2,1)S(1)}, bf16[512,256]{1,0:T(8,128)(2,1)S(1)}, u32[]{:S(2)}, u32[]{:S(2)}) collective-permute-start(bf16[512,256]{1,0:T(8,128)(2,1)S(1)} %get-tuple-element.51), channel_id=1, source_target_pairs={{0,2},{2,0},{4,6},{6,4},{8,10},{10,8},{12,14},{14,12},{1,3},{3,1},... | collective-permute-start | bytes 786440 | tf_op jit(solution)/shard_map/ppermute | solution.py:337
  84.1 42.1 %collective-permute-start.3 = (bf16[512,256]{1,0:T(8,128)(2,1)S(1)}, bf16[512,256]{1,0:T(8,128)(2,1)S(1)}, u32[]{:S(2)}, u32[]{:S(2)}) collective-permute-start(bf16[512,256]{1,0:T(8,128)(2,1)S(1)} %get-tuple-element.49), channel_id=1, source_target_pairs={{0,8},{2,10},{4,12},{6,14},{8,0},{10,2},{12,4},{14,6},{1,9},{3,11}... | collective-permute-start | bytes 786440 | tf_op jit(solution)/shard_map/ppermute | solution.py:337

commit v2 on v1

v2 whole, which is shorter than its diff:
```python
import functools
import math

import jax
import jax.numpy as jnp
from jax import lax
from jax.experimental import pallas as pl
from jax.experimental.pallas import tpu as pltpu
from jax.sharding import PartitionSpec as P

HD = 128
SCALE = HD ** (-0.5) * math.log2(math.e)
MIB = 1024 * 1024
FIELDS = 5
SUM_ROWS = 16
IN_FLIGHT = 5
NEVER = -1e30
ANY = pl.BlockSpec(memory_space=pl.ANY)
SMEM = pl.BlockSpec(memory_space=pltpu.SMEM)
WHOLE = pl.BlockSpec(memory_space=pltpu.VMEM)


def params(*semantics, vmem=24):
    return pltpu.CompilerParams(
        dimension_semantics=semantics or None, vmem_limit_bytes=vmem * MIB
    )


def hint(flops, bytes_accessed, transcendentals):
    return pl.CostEstimate(
        flops=flops, bytes_accessed=bytes_accessed, transcendentals=transcendentals
    )


def arrival_order(groups):
    far = list(range(groups - 1, groups // 2 - 1, -1))
    near = list(range(groups // 2 - 1, 0, -1))
    order = [0]
    for at in range(len(far)):
        order += far[at : at + 1] + near[at : at + 1]
    return order


def write_plan(groups, stored, me, owner_ref, length_ref, table_ref, place_ref, plan_ref):
    pairs = table_ref.shape[1] // groups
    bits = stored.bit_length() - 1

    def slot_of(group, j):
        response = table_ref[j % 2, group * pairs + j // 2]
        slot = owner_ref[response]
        return response, lax.shift_right_logical(slot, bits), slot & (stored - 1)

    for shift in range(groups):
        plan_ref[shift * FIELDS + 3] = 0
        plan_ref[shift * FIELDS + 1] = 0
        row = jnp.int32(0)
        for j in range(2 * pairs):
            _, source, slot_row = slot_of(me ^ shift, j)
            row = jnp.where(source == me, slot_row, row)
        plan_ref[shift * FIELDS] = row
    sources = [slot_of(me, j) for j in range(2 * pairs)]
    for j, (response, source, _) in enumerate(sources):
        shift = source ^ me
        later = place_ref[shift] > place_ref[sources[j ^ 1][1] ^ me]
        plan_ref[shift * FIELDS + 1] = jnp.int32(j // 2)
        plan_ref[shift * FIELDS + 2] = length_ref[response]
        plan_ref[shift * FIELDS + 3] = jnp.int32(1)
        plan_ref[shift * FIELDS + 4] = later.astype(jnp.int32)


def project_rows_kernel(groups, stored, at_ref, owner_ref, length_ref, table_ref, place_ref, x_ref, key_ref, value_ref, out_ref, plan_ref):
    write_plan(groups, stored, at_ref[1], owner_ref, length_ref, table_ref, place_ref, plan_ref)
    width = key_ref.shape[1]
    x = x_ref[...]
    out_ref[:, :width] = jnp.dot(x, key_ref[...], preferred_element_type=jnp.float32)
    out_ref[:, width:] = jnp.dot(x, value_ref[...], preferred_element_type=jnp.float32)


def project_and_plan(rows, key_weight, value_weight, half, width, me, tables, groups, stored):
    total, depth = rows.shape
    block = 256
    weight_spec = pl.BlockSpec((depth, width), lambda i, at: (0, at[0]))
    return pl.pallas_call(
        functools.partial(project_rows_kernel, groups, stored),
        grid_spec=pltpu.PrefetchScalarGridSpec(
            num_scalar_prefetch=1,
            grid=(total // block,),
            in_specs=[SMEM] * len(tables)
            + [pl.BlockSpec((block, depth), lambda i, at: (i, 0)), weight_spec, weight_spec],
            out_specs=[pl.BlockSpec((block, 2 * width), lambda i, at: (i, 0)), SMEM],
        ),
        out_shape=[
            jax.ShapeDtypeStruct((total, 2 * width), jnp.float32),
            jax.ShapeDtypeStruct((groups * FIELDS,), jnp.int32),
        ],
        compiler_params=params("arbitrary", vmem=60),
        cost_estimate=hint(
            4 * total * depth * width, 2 * total * depth + 4 * depth * width + 8 * total * width, 0
        ),
        name="other_half",
    )(jnp.stack([half, me]), *tables, rows, key_weight, value_weight)


def project_kernel(half_ref, x_ref, key_ref, value_ref, *refs):
    out_ref = refs[-1]
    width = key_ref.shape[1]
    x = x_ref[...]
    for at, weight_ref in enumerate((key_ref, value_ref)):
        columns = slice(at * width, (at + 1) * width)
        part = jnp.dot(x, weight_ref[...], preferred_element_type=jnp.float32)

        @pl.when(pl.program_id(0) == 0)
        def _():
            out_ref[:, columns] = part

        @pl.when(pl.program_id(0) > 0)
        def _():
            out_ref[:, columns] += part


def project(rows, key_weight, value_weight, half, width, name, after=()):
    total, depth = rows.shape
    chunk = 1024
    weight_spec = pl.BlockSpec((chunk, width), lambda k, half: (k, half[0]))
    return pl.pallas_call(
        project_kernel,
        grid_spec=pltpu.PrefetchScalarGridSpec(
            num_scalar_prefetch=1,
            grid=(depth // chunk,),
            in_specs=[pl.BlockSpec((total, chunk), lambda k, half: (0, k)), weight_spec, weight_spec]
            + [ANY] * len(after),
            out_specs=pl.BlockSpec((total, 2 * width), lambda k, half: (0, 0)),
        ),
        out_shape=jax.ShapeDtypeStruct((total, 2 * width), jnp.float32),
        compiler_params=params("arbitrary", vmem=48),
        cost_estimate=hint(
            4 * total * depth * width, 2 * total * depth + 4 * depth * width + 8 * total * width, 0
        ),
        name=name,
    )(half[None], rows, key_weight, value_weight, *after)


def finish_kernel(length, width, plan_ref, own_ref, other_ref, *out_refs):
    for shift, out_ref in enumerate(out_refs):
        start = pl.multiple_of(plan_ref[shift * FIELDS] * length, length)
        rows = pl.ds(start, length)
        for at in range(2):
            columns = slice(at * width, (at + 1) * width)
            total = own_ref[rows, columns] + other_ref[rows, columns]
            out_ref[at * length : (at + 1) * length, :] = total.astype(out_ref.dtype)


def finish(plan, own, other, groups, length, name):
    width = own.shape[1] // 2
    return pl.pallas_call(
        functools.partial(finish_kernel, length, width),
        out_shape=[jax.ShapeDtypeStruct((2 * length, width), jnp.bfloat16)] * groups,
        in_specs=[SMEM, WHOLE, WHOLE],
        out_specs=[WHOLE] * groups,
        compiler_params=params(),
        cost_estimate=hint(
            2 * groups * length * width,
            16 * own.shape[0] * width + 4 * groups * length * width,
            0,
        ),
        name=name,
    )(plan, own, other)


def times(a, b):
    return jnp.dot(a, b, preferred_element_type=jnp.float32)


def head_rows(h):
    return slice(h * HD, (h + 1) * HD)


def softmax_part(s, peak):
    return jnp.exp2((s - peak) * SCALE).astype(jnp.bfloat16)


def top_of(s):
    return jnp.max(s, axis=0, keepdims=True)


def rubric_kernel(q_ref, k_ref, v_ref, after_ref, qt_ref, acc_ref, peak_ref, sum_ref):
    heads = qt_ref.shape[1] // HD
    half = k_ref.shape[1] // 2
    keys = k_ref[0]
    values = jnp.concatenate(
        [v_ref[0].T, jnp.ones((SUM_ROWS, 2 * half), jnp.bfloat16)], axis=0
    )
    shape = (half, half)
    causal = lax.broadcasted_iota(jnp.int32, shape, 0) <= lax.broadcasted_iota(jnp.int32, shape, 1)

    def scores(h):
        turned = q_ref[0, :, head_rows(h)].T
        qt_ref[0, head_rows(h), :] = turned
        return times(keys[:half], turned), times(keys[half:], turned[:, half:])

    later = scores(0)
    for h in range(heads):
        first, last = later
        if h + 1 < heads:
            later = scores(h + 1)
        early = jnp.where(causal, first[:, :half], NEVER)
        late = first[:, half:]
        last = jnp.where(causal, last, NEVER)
        early_peak = top_of(early)
        late_peak = jnp.maximum(top_of(late), top_of(last))
        weights = jnp.concatenate(
            [softmax_part(early, early_peak), softmax_part(late, late_peak)], axis=1
        )
        pv = times(values[:, :half], weights)
        more = times(values[:, half:], softmax_part(last, late_peak))
        acc_ref[0, head_rows(h), :half] = pv[:HD, :half]
        acc_ref[0, head_rows(h), half:] = pv[:HD, half:] + more[:HD]
        peak_ref[0, h : h + 1, :half] = early_peak
        peak_ref[0, h : h + 1, half:] = late_peak
        sum_ref[0, h : h + 1, :half] = pv[HD : HD + 1, :half]
        sum_ref[0, h : h + 1, half:] = pv[HD : HD + 1, half:] + more[HD : HD + 1]


def state_shapes(pairs, rows, width):
    heads = width // HD
    return [
        jax.ShapeDtypeStruct((pairs, width, rows), jnp.bfloat16),
        jax.ShapeDtypeStruct((pairs, width, rows), jnp.float32),
        jax.ShapeDtypeStruct((pairs, heads, rows), jnp.float32),
        jax.ShapeDtypeStruct((pairs, heads, rows), jnp.float32),
    ]


def rubric_attention(query, key, value, after):
    pairs, rows, width = query.shape
    steps = key.shape[2] // HD
    step_width = width // steps
    heads = width // HD
    count = key.shape[1]

    def spec(size):
        return pl.BlockSpec((1, size, rows), lambda p, g: (p, g, 0))

    def across(size):
        return pl.BlockSpec((1, rows, size), lambda p, g: (p, 0, g))

    return pl.pallas_call(
        rubric_kernel,
        grid=(pairs, steps),
        in_specs=[across(step_width), across(HD), across(HD), ANY],
        out_specs=[spec(step_width), spec(step_width), spec(heads // steps), spec(heads // steps)],
        out_shape=state_shapes(pairs, rows, width),
        compiler_params=params("arbitrary", "arbitrary"),
        cost_estimate=hint(
            3 * pairs * heads * rows * count * HD,
            pairs * rows * width * 8,
            pairs * heads * rows * count,
        ),
        name="rubric_attention",
    )(query, key, value, after)


def response_kernel(shift, plan_ref, qt_ref, kv_ref, acc_ref, peak_ref, sum_ref, *refs):
    acc_out, peak_out, sum_out, out_ref = refs[-4:]
    heads = qt_ref.shape[1] // HD
    count = kv_ref.shape[0] // 2
    length = plan_ref[shift * FIELDS + 2]
    wanted = plan_ref[shift * FIELDS + 3] == 1
    completes = plan_ref[shift * FIELDS + 4] == 1

    @pl.when(wanted)
    def _():
        live_rows = lax.broadcasted_iota(jnp.int32, (count, HD), 0) < length
        live_columns = lax.broadcasted_iota(jnp.int32, (HD + SUM_ROWS, count), 1) < length
        block = kv_ref[:count, :].astype(jnp.float32)
        keys = jnp.where(live_rows, block, block[0:1]).astype(jnp.bfloat16)
        values = jnp.concatenate(
            [kv_ref[count:, :].astype(jnp.float32).T, jnp.ones((SUM_ROWS, count), jnp.float32)],
            axis=0,
        )
        values = jnp.where(live_columns, values, 0.0).astype(jnp.bfloat16)
        later = times(keys, qt_ref[0, head_rows(0), :])
        for h in range(heads):
            s = later
            if h + 1 < heads:
                later = times(keys, qt_ref[0, head_rows(h + 1), :])
            old_peak = peak_ref[0, h : h + 1, :]
            peak = jnp.maximum(old_peak, top_of(s))
            fade = jnp.exp2((old_peak - peak) * SCALE)
            pv = times(values, softmax_part(s, peak))
            acc_out[0, head_rows(h), :] = acc_ref[0, head_rows(h), :] * fade + pv[:HD]
            peak_out[0, h : h + 1, :] = peak
            sum_out[0, h : h + 1, :] = sum_ref[0, h : h + 1, :] * fade + pv[HD : HD + 1]

    @pl.when(jnp.logical_not(wanted))
    def _():
        acc_out[...] = acc_ref[...]
        peak_out[...] = peak_ref[...]
        sum_out[...] = sum_ref[...]

    @pl.when(completes | jnp.logical_not(wanted))
    def _():
        for h in range(heads):
            share = acc_out[0, head_rows(h), :] * (1.0 / sum_out[0, h : h + 1, :])
            out_ref[0, :, head_rows(h)] = share.astype(out_ref.dtype).T


def response_attention(shift, plan, kv, state, out):
    pairs, width, rows = state[0].shape
    heads = width // HD
    steps = kv.shape[1] // HD
    step_width = width // steps
    count = kv.shape[0] // 2
    pair_at = shift * FIELDS + 1

    def spec(size):
        return pl.BlockSpec((1, size, rows), lambda g, plan: (plan[pair_at], g, 0))

    state_specs = [spec(step_width), spec(heads // steps), spec(heads // steps)]
    operands = [plan, state[0], kv, *state[1:]]
    in_specs = [
        spec(step_width),
        pl.BlockSpec((2 * count, HD), lambda g, plan: (0, g)),
        *state_specs,
    ]
    aliases = {3: 0, 4: 1, 5: 2}
    if out is not None:
        aliases[len(operands)] = 3
        operands.append(out)
        in_specs.append(ANY)
    results = pl.pallas_call(
        functools.partial(response_kernel, shift),
        grid_spec=pltpu.PrefetchScalarGridSpec(
            num_scalar_prefetch=1,
            grid=(steps,),
            in_specs=in_specs,
            out_specs=state_specs
            + [pl.BlockSpec((1, rows, step_width), lambda g, plan: (plan[pair_at], 0, g))],
        ),
        out_shape=state_shapes(pairs, rows, width)[1:]
        + [jax.ShapeDtypeStruct((pairs, rows, width), jnp.bfloat16)],
        input_output_aliases=aliases,
        compiler_params=params("arbitrary"),
        cost_estimate=hint(
            4 * heads * rows * count * HD, rows * width * 12, heads * rows * count
        ),
        name="response_attention",
    )(*operands)
    return [state[0], *results[:3]], results[3]


def local(
    rubric_query,
    rubric_key,
    rubric_value,
    response_states,
    key_weight,
    value_weight,
    owner_slot,
    response_length,
    pair_table,
):
    groups = lax.axis_size("dp")
    stored, length, depth = response_states.shape
    tensor = lax.axis_size("tensor")
    width = key_weight.shape[1] // tensor
    me = lax.axis_index("dp").astype(jnp.int32)
    own_half = lax.axis_index("tensor").astype(jnp.int32)
    other_half = 1 - own_half
    rows = response_states.reshape(stored * length, depth)
    swap = [(0, 1), (1, 0)]
    order = arrival_order(groups)
    place = jnp.array([order.index(shift) for shift in range(groups)], jnp.int32)
    tables = [owner_slot, response_length, pair_table.T, place]

    other, plan = project_and_plan(
        rows, key_weight, value_weight, other_half, width, me, tables, groups, stored
    )
    received = lax.ppermute(other, "tensor", swap)
    own = project(rows, key_weight, value_weight, own_half, width, "own_half", after=[plan])
    blocks = finish(plan, own, received, groups, length, "finish")
    arrived = {0: blocks[0]}

    def send(shift, *after):
        block = lax.optimization_barrier((blocks[shift], *after))[0]
        arrived[shift] = lax.ppermute(block, "dp", [(g, g ^ shift) for g in range(groups)])

    for shift in order[1 : IN_FLIGHT + 1]:
        send(shift)
    state = rubric_attention(rubric_query, rubric_key, rubric_value, blocks[0])
    out = None
    for at, shift in enumerate(order):
        if at and at + IN_FLIGHT < len(order):
            send(order[at + IN_FLIGHT], arrived[shift], state[2])
        state, out = response_attention(shift, plan, arrived[shift], state, out)
    return out


def solution(mesh):
    return jax.shard_map(
        local,
        mesh=mesh,
        in_specs=(
            P(("rep", "dp"), None, "tensor"),
            P(("rep", "dp"), None, "tensor"),
            P(("rep", "dp"), None, "tensor"),
            P(("rep", "dp"), None, "tensor"),
            P("tensor", None),
            P("tensor", None),
            P("rep"),
            P("rep"),
            P("rep", None),
        ),
        out_specs=P(("rep", "dp"), None, "tensor"),
        check_vma=False,
    )
```

time: 135 us -> 92.9 us (0.69)
  the two profiles are of different devices: /device:TPU:0 before, /device:TPU:16 now
where the time goes in v2:
time: 92.9 us; the launch traced here: 92.7 us
  Pallas kernels  68.1 us (73%)
  waiting for transfers between devices  12.4 us (13%)
  starting transfers between devices  10.8 us (12%)
    pallas_call x8, Pallas kernels, response_attention(): pl.pallas_call(functools.partial(response_kernel, shift), grid_spec=pltpu...  32.9 us
    pallas_call x1, Pallas kernels, project(): pl.pallas_call(project_kernel, grid_spec=pltpu.PrefetchScalarGridSpec(num...  12.9 us
    ppermute x7, waiting for transfers between devices, send(): lax.ppermute(block, 'dp', [(g, g ^ shift) for g in range(groups)])  12.4 us
    pallas_call x1, Pallas kernels, rubric_attention(): pl.pallas_call(rubric_kernel, grid=(pairs, steps), in_specs=[across(step_...  11.2 us
    ppermute x7, starting transfers between devices, send(): lax.ppermute(block, 'dp', [(g, g ^ shift) for g in range(groups)])  10.8 us
    pallas_call x1, Pallas kernels, project_and_plan(): pl.pallas_call(functools.partial(project_rows_kernel, groups, stored), gr...  10.1 us
  transfers between devices with their start and end apart: 8, of which 1 were waited for; matrix products, arithmetic and copies ran while one was open for 0% of the time, Pallas kernels for 57%

profile of v2, /device:TPU:16, one launch (start us, length us, event | category | flops | bytes accessed | tf_op | source)
XLA Modules:
  0.0 92.7 jit_solution(8985383035286518831)
XLA Ops:
  0.0 0.6 pad_add_fusion.at_ref
  0.6 10.1 %other_half.1 = (f32[1024,512]{1,0:T(8,128)}, s32[40]{0:T(128)}) custom-call(s32[2]{0:T(128)} %pad_add_fusion.at_ref, s32[32]{0:T(128)} %owner_ref.1, s32[32]{0:T(128)} %length_ref.1, s32[2,32]{1,0:T(2,128)} %bitcast.7, s32[8]{0:T(128)} %constant.12.clone.place_ref, bf16[1024,4096]{1,0:T(8,128)(2,1)} %bitcast.5, bf16[4096,512]{1,0:T(8,128)(2,1)} %key_ref.3, ...), custom_call_target="tpu_custom_call" | custom-call | flops 4294967296 | bytes 14680064 | tf_op jit(solution)/shard_map/other_half/pallas_call | solution.py:83
  10.7 0.0 collective-permute-start
  10.7 0.7 copy-done
  11.4 12.9 %own_half.1.own_ref = f32[1024,512]{1,0:T(8,128)S(1)} custom-call(s32[1]{0:T(128)} %bitcast.4.half_ref, bf16[1024,4096]{1,0:T(8,128)(2,1)} %bitcast.6, bf16[4096,512]{1,0:T(8,128)(2,1)} %key_ref.3, bf16[4096,512]{1,0:T(8,128)(2,1)} %value_ref.3, s32[40]{0:T(128)S(1)} %copy-done), custom_call_target="tpu_custom_call" | custom-call | flops 4294967296 | bytes 14680064 | tf_op jit(solution)/shard_map/own_half/pallas_call | solution.py:125
  24.3 0.0 copy-start.2
  24.3 0.0 collective-permute-done.other_ref
  24.3 1.0 %finish.1 = (bf16[512,256]{1,0:T(8,128)(2,1)S(1)}, bf16[512,256]{1,0:T(8,128)(2,1)S(1)}, bf16[512,256]{1,0:T(8,128)(2,1)S(1)}, bf16[512,256]{1,0:T(8,128)(2,1)S(...) custom-call(s32[40]{0:T(128)S(1)} %copy-done, ...), custom_call_target="tpu_custom_call" | custom-call | flops 1048576 | bytes 6291456 | tf_op jit(solution)/shard_map/finish/pallas_call | solution.py:155
  25.4 1.5 %collective-permute-start.2 = (bf16[512,256]{1,0:T(8,128)(2,1)S(1)}, bf16[512,256]{1,0:T(8,128)(2,1)S(1)}, u32[]{:S(2)}, u32[]{:S(2)}) collective-permute-start(bf16[512,256]{1,0:T(8,128)(2,1)S(1)} %get-tuple-element.56), channel_id=1, source_target_pairs={{0,14},{2,12},{4,10},{6,8},{8,6},{10,4},{12,2},{14,0},{1,15},{3,13... | collective-permute-start | bytes 786440 | tf_op jit(solution)/shard_map/ppermute | solution.py:386
  26.8 1.2 %collective-permute-start.1 = (bf16[512,256]{1,0:T(8,128)(2,1)S(1)}, bf16[512,256]{1,0:T(8,128)(2,1)S(1)}, u32[]{:S(2)}, u32[]{:S(2)}) collective-permute-start(bf16[512,256]{1,0:T(8,128)(2,1)S(1)} %get-tuple-element.55), channel_id=1, source_target_pairs={{0,6},{2,4},{4,2},{6,0},{8,14},{10,12},{12,10},{14,8},{1,7},{3,5},... | collective-permute-start | bytes 786440 | tf_op jit(solution)/shard_map/ppermute | solution.py:386
  28.0 2.7 %collective-permute-start.5 = (bf16[512,256]{1,0:T(8,128)(2,1)S(1)}, bf16[512,256]{1,0:T(8,128)(2,1)S(1)}, u32[]{:S(2)}, u32[]{:S(2)}) collective-permute-start(bf16[512,256]{1,0:T(8,128)(2,1)S(1)} %get-tuple-element.68), channel_id=1, source_target_pairs={{0,10},{2,8},{4,14},{6,12},{8,2},{10,0},{12,6},{14,4},{1,11},{3,9}... | collective-permute-start | bytes 786440 | tf_op jit(solution)/shard_map/ppermute | solution.py:386
  30.8 2.5 %collective-permute-start.6 = (bf16[512,256]{1,0:T(8,128)(2,1)S(1)}, bf16[512,256]{1,0:T(8,128)(2,1)S(1)}, u32[]{:S(2)}, u32[]{:S(2)}) collective-permute-start(bf16[512,256]{1,0:T(8,128)(2,1)S(1)} %get-tuple-element.69), channel_id=1, source_target_pairs={{0,4},{2,6},{4,0},{6,2},{8,12},{10,14},{12,8},{14,10},{1,5},{3,7},... | collective-permute-start | bytes 786440 | tf_op jit(solution)/shard_map/ppermute | solution.py:386
  33.3 11.2 %rubric_attention.1 = (bf16[4,2048,256]{2,1,0:T(8,128)(2,1)S(1)}, f32[4,2048,256]{2,1,0:T(8,128)S(1)}, f32[4,16,256]{2,1,0:T(8,128)S(1)}, f32[4,16,256]{2,1,0:T(8,128)S(1)}) custom-call(bf16[4,256,2048]{2,1,0:T(8,128)(2,1)S(1)} %copy-done.2, bf16[4,256,256]{2,1,0:T(8,128)(2,1)S(1)} %copy-done.3, bf16[4,256,256]{2,1,0:T(8,128)(2,1)S(1)} %copy-done.4, ...), custom_call_target="tpu_custom_call" | custom-call | flops 1610612736 | bytes 16777216 | tf_op jit(solution)/shard_map/rubric_attention/pallas_call | solution.py:247
  44.5 3.9 %response_attention.8 = (f32[4,2048,256]{2,1,0:T(8,128)S(1)}, f32[4,16,256]{2,1,0:T(8,128)S(1)}, f32[4,16,256]{2,1,0:T(8,128)S(1)}, bf16[4,256,2048]{2,1,0:T(8,128)(2,1)}) custom-call(s32[40]{0:T(128)S(1)} %copy-done.1, bf16[4,2048,256]{2,1,0:T(8,128)(2,1)S(1)} %get-tuple-element.53.qt_ref, ...), custom_call_target="tpu_custom_call", output_to_operand_aliasing={{0}: (3, {}), {1}: (4, {}), {2}: (5, {})} | custom-call | flops 536870912 | bytes 6291456 | tf_op jit(solution)/shard_map/response_attention/pallas_call | solution.py:331
  48.4 0.5 collective-permute-start.4
  48.9 3.9 %response_attention.9 = (f32[4,2048,256]{2,1,0:T(8,128)S(1)}, f32[4,16,256]{2,1,0:T(8,128)S(1)}, f32[4,16,256]{2,1,0:T(8,128)S(1)}, bf16[4,256,2048]{2,1,0:T(8,128)(2,1)}) custom-call(s32[40]{0:T(128)S(1)} %copy-done.1, bf16[4,2048,256]{2,1,0:T(8,128)(2,1)S(1)} %get-tuple-element.53.qt_ref, ...), custom_call_target="tpu_custom_call", output_to_operand_aliasing={{0}: (3, {}), {1}: (4, {}), {2}: (5, {}), {3}: (6, {})} | custom-call | flops 536870912 | bytes 6291456 | tf_op jit(solution)/shard_map/response_attention/pallas_call | solution.py:331
  52.8 2.4 %collective-permute-start.3 = (bf16[512,256]{1,0:T(8,128)(2,1)S(1)}, bf16[512,256]{1,0:T(8,128)(2,1)S(1)}, u32[]{:S(2)}, u32[]{:S(2)}) collective-permute-start(bf16[512,256]{1,0:T(8,128)(2,1)S(1)} %get-tuple-element.65), channel_id=1, source_target_pairs={{0,8},{2,10},{4,12},{6,14},{8,0},{10,2},{12,4},{14,6},{1,9},{3,11}... | collective-permute-start | bytes 786440 | tf_op jit(solution)/shard_map/ppermute | solution.py:386
  55.2 3.9 %response_attention.10 = (f32[4,2048,256]{2,1,0:T(8,128)S(1)}, f32[4,16,256]{2,1,0:T(8,128)S(1)}, f32[4,16,256]{2,1,0:T(8,128)S(1)}, bf16[4,256,2048]{2,1,0:T(8,128)(2,1)}) custom-call(s32[40]{0:T(128)S(1)} %copy-done.1, bf16[4,2048,256]{2,1,0:T(8,128)(2,1)S(1)} %get-tuple-element.53.qt_ref, ...), custom_call_target="tpu_custom_call", output_to_operand_aliasing={{0}: (3, {}), {1}: (4, {}), {2}: (5, {}), {3}: (6, {})} | custom-call | flops 536870912 | bytes 6291456 | tf_op jit(solution)/shard_map/response_attention/pallas_call | solution.py:331
  59.0 12.4 %collective-permute-done.7.kv_ref = bf16[512,256]{1,0:T(8,128)(2,1)S(1)} collective-permute-done((bf16[512,256]{1,0:T(8,128)(2,1)S(1)}, bf16[512,256]{1,0:T(8,128)(2,1)S(1)}, u32[]{:S(2)}, u32[]{:S(2)}) %collective-permute-start.7) | collective-permute-done | bytes 262176 | tf_op jit(solution)/shard_map/ppermute | solution.py:386
  71.4 4.3 %response_attention.11 = (f32[4,2048,256]{2,1,0:T(8,128)S(1)}, f32[4,16,256]{2,1,0:T(8,128)S(1)}, f32[4,16,256]{2,1,0:T(8,128)S(1)}, bf16[4,256,2048]{2,1,0:T(8,128)(2,1)}) custom-call(s32[40]{0:T(128)S(1)} %copy-done.1, bf16[4,2048,256]{2,1,0:T(8,128)(2,1)S(1)} %get-tuple-element.53.qt_ref, ...), custom_call_target="tpu_custom_call", output_to_operand_aliasing={{0}: (3, {}), {1}: (4, {}), {2}: (5, {}), {3}: (6, {})} | custom-call | flops 536870912 | bytes 6291456 | tf_op jit(solution)/shard_map/response_attention/pallas_call | solution.py:331
  75.7 4.3 %response_attention.12 = (f32[4,2048,256]{2,1,0:T(8,128)S(1)}, f32[4,16,256]{2,1,0:T(8,128)S(1)}, f32[4,16,256]{2,1,0:T(8,128)S(1)}, bf16[4,256,2048]{2,1,0:T(8,128)(2,1)}) custom-call(s32[40]{0:T(128)S(1)} %copy-done.1, bf16[4,2048,256]{2,1,0:T(8,128)(2,1)S(1)} %get-tuple-element.53.qt_ref, ...), custom_call_target="tpu_custom_call", output_to_operand_aliasing={{0}: (3, {}), {1}: (4, {}), {2}: (5, {}), {3}: (6, {})} | custom-call | flops 536870912 | bytes 6291456 | tf_op jit(solution)/shard_map/response_attention/pallas_call | solution.py:331
  80.0 4.1 %response_attention.13 = (f32[4,2048,256]{2,1,0:T(8,128)S(1)}, f32[4,16,256]{2,1,0:T(8,128)S(1)}, f32[4,16,256]{2,1,0:T(8,128)S(1)}, bf16[4,256,2048]{2,1,0:T(8,128)(2,1)}) custom-call(s32[40]{0:T(128)S(1)} %copy-done.1, bf16[4,2048,256]{2,1,0:T(8,128)(2,1)S(1)} %get-tuple-element.53.qt_ref, ...), custom_call_target="tpu_custom_call", output_to_operand_aliasing={{0}: (3, {}), {1}: (4, {}), {2}: (5, {}), {3}: (6, {})} | custom-call | flops 536870912 | bytes 6291456 | tf_op jit(solution)/shard_map/response_attention/pallas_call | solution.py:331
  84.1 4.3 %response_attention.14 = (f32[4,2048,256]{2,1,0:T(8,128)S(1)}, f32[4,16,256]{2,1,0:T(8,128)S(1)}, f32[4,16,256]{2,1,0:T(8,128)S(1)}, bf16[4,256,2048]{2,1,0:T(8,128)(2,1)}) custom-call(s32[40]{0:T(128)S(1)} %copy-done.1, bf16[4,2048,256]{2,1,0:T(8,128)(2,1)S(1)} %get-tuple-element.53.qt_ref, ...), custom_call_target="tpu_custom_call", output_to_operand_aliasing={{0}: (3, {}), {1}: (4, {}), {2}: (5, {}), {3}: (6, {})} | custom-call | flops 536870912 | bytes 6291456 | tf_op jit(solution)/shard_map/response_attention/pallas_call | solution.py:331
  88.4 4.3 %response_attention.15 = (f32[4,2048,256]{2,1,0:T(8,128)S(1)}, f32[4,16,256]{2,1,0:T(8,128)S(1)}, f32[4,16,256]{2,1,0:T(8,128)S(1)}, bf16[4,256,2048]{2,1,0:T(8,128)(2,1)}) custom-call(s32[40]{0:T(128)S(1)} %copy-done.1, bf16[4,2048,256]{2,1,0:T(8,128)(2,1)S(1)} %get-tuple-element.53.qt_ref, ...), custom_call_target="tpu_custom_call", output_to_operand_aliasing={{0}: (3, {}), {1}: (4, {}), {2}: (5, {}), {3}: (6, {})} | custom-call | flops 536870912 | bytes 6291456 | tf_op jit(solution)/shard_map/response_attention/pallas_call | solution.py:331
  (15 shorter events, 0.0 us)
Async XLA Ops:
  10.7 13.6 %collective-permute-start = (f32[1024,512]{1,0:T(8,128)}, f32[1024,512]{1,0:T(8,128)S(1)}, u32[]{:S(2)}, u32[]{:S(2)}) collective-permute-start(f32[1024,512]{1,0:T(8,128)} %get-tuple-element.51), channel_id=1, source_target_pairs={{0,1},{1,0},{2,3},{3,2},{4,5},{5,4},{6,7},{7,6},{8,9},{9,8},{10,11... | collective-permute-start | bytes 6291464 | tf_op jit(solution)/shard_map/ppermute | solution.py:379
  10.7 0.7 copy-start
  11.4 21.8 %copy-start.3 = (bf16[4,256,256]{2,1,0:T(8,128)(2,1)S(1)}, bf16[4,256,256]{2,1,0:T(8,128)(2,1)}, u32[]{:S(2)}) copy-start(bf16[4,256,256]{2,1,0:T(8,128)(2,1)} %k_ref.1) | copy-start | bytes 1572868
  11.4 21.8 %copy-start.4 = (bf16[4,256,256]{2,1,0:T(8,128)(2,1)S(1)}, bf16[4,256,256]{2,1,0:T(8,128)(2,1)}, u32[]{:S(2)}) copy-start(bf16[4,256,256]{2,1,0:T(8,128)(2,1)} %v_ref.1) | copy-start | bytes 1572868
  24.3 9.0 %copy-start.2 = (bf16[4,256,2048]{2,1,0:T(8,128)(2,1)S(1)}, bf16[4,256,2048]{2,1,0:T(8,128)(2,1)}, u32[]{:S(2)}) copy-start(bf16[4,256,2048]{2,1,0:T(8,128)(2,1)} %q_ref.1) | copy-start | bytes 12582916
  25.3 19.2 %copy-start.1 = (s32[40]{0:T(128)S(1)}, s32[40]{0:T(128)}, u32[]{:S(2)}) copy-start(s32[40]{0:T(128)} %get-tuple-element.50.refs_0_.plan_ref) | copy-start | bytes 484
  25.4 23.0 %collective-permute-start.2 = (bf16[512,256]{1,0:T(8,128)(2,1)S(1)}, bf16[512,256]{1,0:T(8,128)(2,1)S(1)}, u32[]{:S(2)}, u32[]{:S(2)}) collective-permute-start(bf16[512,256]{1,0:T(8,128)(2,1)S(1)} %get-tuple-element.56), channel_id=1, source_target_pairs={{0,14},{2,12},{4,10},{6,8},{8,6},{10,4},{12,2},{14,0},{1,15},{3,13... | collective-permute-start | bytes 786440 | tf_op jit(solution)/shard_map/ppermute | solution.py:386
  26.8 25.9 %collective-permute-start.1 = (bf16[512,256]{1,0:T(8,128)(2,1)S(1)}, bf16[512,256]{1,0:T(8,128)(2,1)S(1)}, u32[]{:S(2)}, u32[]{:S(2)}) collective-permute-start(bf16[512,256]{1,0:T(8,128)(2,1)S(1)} %get-tuple-element.55), channel_id=1, source_target_pairs={{0,6},{2,4},{4,2},{6,0},{8,14},{10,12},{12,10},{14,8},{1,7},{3,5},... | collective-permute-start | bytes 786440 | tf_op jit(solution)/shard_map/ppermute | solution.py:386
  28.0 52.0 %collective-permute-start.5 = (bf16[512,256]{1,0:T(8,128)(2,1)S(1)}, bf16[512,256]{1,0:T(8,128)(2,1)S(1)}, u32[]{:S(2)}, u32[]{:S(2)}) collective-permute-start(bf16[512,256]{1,0:T(8,128)(2,1)S(1)} %get-tuple-element.68), channel_id=1, source_target_pairs={{0,10},{2,8},{4,14},{6,12},{8,2},{10,0},{12,6},{14,4},{1,11},{3,9}... | collective-permute-start | bytes 786440 | tf_op jit(solution)/shard_map/ppermute | solution.py:386
  30.8 45.0 %collective-permute-start.6 = (bf16[512,256]{1,0:T(8,128)(2,1)S(1)}, bf16[512,256]{1,0:T(8,128)(2,1)S(1)}, u32[]{:S(2)}, u32[]{:S(2)}) collective-permute-start(bf16[512,256]{1,0:T(8,128)(2,1)S(1)} %get-tuple-element.69), channel_id=1, source_target_pairs={{0,4},{2,6},{4,0},{6,2},{8,12},{10,14},{12,8},{14,10},{1,5},{3,7},... | collective-permute-start | bytes 786440 | tf_op jit(solution)/shard_map/ppermute | solution.py:386
  33.2 38.2 %collective-permute-start.7 = (bf16[512,256]{1,0:T(8,128)(2,1)S(1)}, bf16[512,256]{1,0:T(8,128)(2,1)S(1)}, u32[]{:S(2)}, u32[]{:S(2)}) collective-permute-start(bf16[512,256]{1,0:T(8,128)(2,1)S(1)} %get-tuple-element.70), channel_id=1, source_target_pairs={{0,12},{2,14},{4,8},{6,10},{8,4},{10,6},{12,0},{14,2},{1,13},{3,15... | collective-permute-start | bytes 786440 | tf_op jit(solution)/shard_map/ppermute | solution.py:386
  48.4 35.7 %collective-permute-start.4 = (bf16[512,256]{1,0:T(8,128)(2,1)S(1)}, bf16[512,256]{1,0:T(8,128)(2,1)S(1)}, u32[]{:S(2)}, u32[]{:S(2)}) collective-permute-start(bf16[512,256]{1,0:T(8,128)(2,1)S(1)} %get-tuple-element.67), channel_id=1, source_target_pairs={{0,2},{2,0},{4,6},{6,4},{8,10},{10,8},{12,14},{14,12},{1,3},{3,1},... | collective-permute-start | bytes 786440 | tf_op jit(solution)/shard_map/ppermute | solution.py:386
  52.8 35.6 %collective-permute-start.3 = (bf16[512,256]{1,0:T(8,128)(2,1)S(1)}, bf16[512,256]{1,0:T(8,128)(2,1)S(1)}, u32[]{:S(2)}, u32[]{:S(2)}) collective-permute-start(bf16[512,256]{1,0:T(8,128)(2,1)S(1)} %get-tuple-element.65), channel_id=1, source_target_pairs={{0,8},{2,10},{4,12},{6,14},{8,0},{10,2},{12,4},{14,6},{1,9},{3,11}... | collective-permute-start | bytes 786440 | tf_op jit(solution)/shard_map/ppermute | solution.py:386

commit v3 on v2

--- a/solution.py
+++ b/solution.py
@@ -13,7 +13,7 @@
 MIB = 1024 * 1024
 FIELDS = 5
 SUM_ROWS = 16
-IN_FLIGHT = 5
+SUB_ROWS = 128
 NEVER = -1e30
 ANY = pl.BlockSpec(memory_space=pl.ANY)
 SMEM = pl.BlockSpec(memory_space=pltpu.SMEM)
@@ -35,7 +35,7 @@
 def arrival_order(groups):
     far = list(range(groups - 1, groups // 2 - 1, -1))
     near = list(range(groups // 2 - 1, 0, -1))
-    order = [0]
+    order = []
     for at in range(len(far)):
         order += far[at : at + 1] + near[at : at + 1]
     return order
@@ -68,26 +68,27 @@
         plan_ref[shift * FIELDS + 4] = later.astype(jnp.int32)
 
 
-def project_rows_kernel(groups, stored, at_ref, owner_ref, length_ref, table_ref, place_ref, x_ref, key_ref, value_ref, out_ref, plan_ref):
-    write_plan(groups, stored, at_ref[1], owner_ref, length_ref, table_ref, place_ref, plan_ref)
+def project_rows_kernel(groups, stored, half_ref, me_ref, owner_ref, length_ref, table_ref, place_ref, x_ref, key_ref, value_ref, out_ref, plan_ref):
+    write_plan(groups, stored, me_ref[0], owner_ref, length_ref, table_ref, place_ref, plan_ref)
     width = key_ref.shape[1]
-    x = x_ref[...]
-    out_ref[:, :width] = jnp.dot(x, key_ref[...], preferred_element_type=jnp.float32)
-    out_ref[:, width:] = jnp.dot(x, value_ref[...], preferred_element_type=jnp.float32)
+    for at in range(0, x_ref.shape[0], SUB_ROWS):
+        part = slice(at, at + SUB_ROWS)
+        out_ref[part, :width] = times(x_ref[part, :], key_ref[...])
+        out_ref[part, width:] = times(x_ref[part, :], value_ref[...])
 
 
 def project_and_plan(rows, key_weight, value_weight, half, width, me, tables, groups, stored):
     total, depth = rows.shape
     block = 256
-    weight_spec = pl.BlockSpec((depth, width), lambda i, at: (0, at[0]))
+    weight_spec = pl.BlockSpec((depth, width), lambda i, half, me: (0, half[0]))
     return pl.pallas_call(
         functools.partial(project_rows_kernel, groups, stored),
         grid_spec=pltpu.PrefetchScalarGridSpec(
-            num_scalar_prefetch=1,
+            num_scalar_prefetch=2,
             grid=(total // block,),
             in_specs=[SMEM] * len(tables)
-            + [pl.BlockSpec((block, depth), lambda i, at: (i, 0)), weight_spec, weight_spec],
-            out_specs=[pl.BlockSpec((block, 2 * width), lambda i, at: (i, 0)), SMEM],
+            + [pl.BlockSpec((block, depth), lambda i, half, me: (i, 0)), weight_spec, weight_spec],
+            out_specs=[pl.BlockSpec((block, 2 * width), lambda i, half, me: (i, 0)), SMEM],
         ),
         out_shape=[
             jax.ShapeDtypeStruct((total, 2 * width), jnp.float32),
@@ -98,73 +99,33 @@
             4 * total * depth * width, 2 * total * depth + 4 * depth * width + 8 * total * width, 0
         ),
         name="other_half",
-    )(jnp.stack([half, me]), *tables, rows, key_weight, value_weight)
-
-
-def project_kernel(half_ref, x_ref, key_ref, value_ref, *refs):
-    out_ref = refs[-1]
-    width = key_ref.shape[1]
-    x = x_ref[...]
-    for at, weight_ref in enumerate((key_ref, value_ref)):
-        columns = slice(at * width, (at + 1) * width)
-        part = jnp.dot(x, weight_ref[...], preferred_element_type=jnp.float32)
-
-        @pl.when(pl.program_id(0) == 0)
-        def _():
-            out_ref[:, columns] = part
-
-        @pl.when(pl.program_id(0) > 0)
-        def _():
-            out_ref[:, columns] += part
-
-
-def project(rows, key_weight, value_weight, half, width, name, after=()):
-    total, depth = rows.shape
-    chunk = 1024
-    weight_spec = pl.BlockSpec((chunk, width), lambda k, half: (k, half[0]))
-    return pl.pallas_call(
-        project_kernel,
-        grid_spec=pltpu.PrefetchScalarGridSpec(
-            num_scalar_prefetch=1,
-            grid=(depth // chunk,),
-            in_specs=[pl.BlockSpec((total, chunk), lambda k, half: (0, k)), weight_spec, weight_spec]
-            + [ANY] * len(after),
-            out_specs=pl.BlockSpec((total, 2 * width), lambda k, half: (0, 0)),
-        ),
-        out_shape=jax.ShapeDtypeStruct((total, 2 * width), jnp.float32),
-        compiler_params=params("arbitrary", vmem=48),
-        cost_estimate=hint(
-            4 * total * depth * width, 2 * total * depth + 4 * depth * width + 8 * total * width, 0
-        ),
-        name=name,
-    )(half[None], rows, key_weight, value_weight, *after)
-
-
-def finish_kernel(length, width, plan_ref, own_ref, other_ref, *out_refs):
+    )(half[None], me[None], *tables, rows, key_weight, value_weight)
+
+
+def finish_kernel(length, width, plan_ref, own_keys_ref, own_values_ref, other_ref, *out_refs):
     for shift, out_ref in enumerate(out_refs):
         start = pl.multiple_of(plan_ref[shift * FIELDS] * length, length)
         rows = pl.ds(start, length)
-        for at in range(2):
-            columns = slice(at * width, (at + 1) * width)
-            total = own_ref[rows, columns] + other_ref[rows, columns]
+        for at, own_ref in enumerate((own_keys_ref, own_values_ref)):
+            total = own_ref[rows, :] + other_ref[rows, at * width : (at + 1) * width]
             out_ref[at * length : (at + 1) * length, :] = total.astype(out_ref.dtype)
 
 
-def finish(plan, own, other, groups, length, name):
-    width = own.shape[1] // 2
+def finish(plan, own_keys, own_values, other, groups, length, name):
+    total, width = own_keys.shape
     return pl.pallas_call(
         functools.partial(finish_kernel, length, width),
         out_shape=[jax.ShapeDtypeStruct((2 * length, width), jnp.bfloat16)] * groups,
-        in_specs=[SMEM, WHOLE, WHOLE],
+        in_specs=[SMEM, WHOLE, WHOLE, WHOLE],
         out_specs=[WHOLE] * groups,
         compiler_params=params(),
         cost_estimate=hint(
             2 * groups * length * width,
-            16 * own.shape[0] * width + 4 * groups * length * width,
+            16 * total * width + 4 * groups * length * width,
             0,
         ),
         name=name,
-    )(plan, own, other)
+    )(plan, own_keys, own_values, other)
 
 
 def times(a, b):
@@ -183,7 +144,8 @@
     return jnp.max(s, axis=0, keepdims=True)
 
 
-def rubric_kernel(q_ref, k_ref, v_ref, after_ref, qt_ref, acc_ref, peak_ref, sum_ref):
+def rubric_kernel(q_ref, k_ref, v_ref, *refs):
+    qt_ref, acc_ref, peak_ref, sum_ref = refs[-4:]
     heads = qt_ref.shape[1] // HD
     half = k_ref.shape[1] // 2
     keys = k_ref[0]
@@ -231,7 +193,7 @@
     ]
 
 
-def rubric_attention(query, key, value, after):
+def rubric_attention(first, some, query, key, value, state, after):
     pairs, rows, width = query.shape
     steps = key.shape[2] // HD
     step_width = width // steps
@@ -239,25 +201,26 @@
     count = key.shape[1]
 
     def spec(size):
-        return pl.BlockSpec((1, size, rows), lambda p, g: (p, g, 0))
+        return pl.BlockSpec((1, size, rows), lambda p, g: (first + p, g, 0))
 
     def across(size):
-        return pl.BlockSpec((1, rows, size), lambda p, g: (p, 0, g))
+        return pl.BlockSpec((1, rows, size), lambda p, g: (first + p, 0, g))
 
     return pl.pallas_call(
         rubric_kernel,
-        grid=(pairs, steps),
-        in_specs=[across(step_width), across(HD), across(HD), ANY],
+        grid=(some, steps),
+        in_specs=[across(step_width), across(HD), across(HD)] + [ANY] * (1 + len(state)),
         out_specs=[spec(step_width), spec(step_width), spec(heads // steps), spec(heads // steps)],
         out_shape=state_shapes(pairs, rows, width),
+        input_output_aliases={4 + i: i for i in range(len(state))},
         compiler_params=params("arbitrary", "arbitrary"),
         cost_estimate=hint(
-            3 * pairs * heads * rows * count * HD,
-            pairs * rows * width * 8,
-            pairs * heads * rows * count,
+            3 * some * heads * rows * count * HD,
+            some * rows * width * 8,
+            some * heads * rows * count,
         ),
         name="rubric_attention",
-    )(query, key, value, after)
+    )(query, key, value, after, *state)
 
 
 def response_kernel(shift, plan_ref, qt_ref, kv_ref, acc_ref, peak_ref, sum_ref, *refs):
@@ -362,6 +325,7 @@
 ):
     groups = lax.axis_size("dp")
     stored, length, depth = response_states.shape
+    pairs = rubric_query.shape[0]
     tensor = lax.axis_size("tensor")
     width = key_weight.shape[1] // tensor
     me = lax.axis_index("dp").astype(jnp.int32)
@@ -370,29 +334,39 @@
     rows = response_states.reshape(stored * length, depth)
     swap = [(0, 1), (1, 0)]
     order = arrival_order(groups)
-    place = jnp.array([order.index(shift) for shift in range(groups)], jnp.int32)
+    place = jnp.array([0] + [1 + order.index(s) for s in range(1, groups)], jnp.int32)
     tables = [owner_slot, response_length, pair_table.T, place]
 
     other, plan = project_and_plan(
         rows, key_weight, value_weight, other_half, width, me, tables, groups, stored
     )
     received = lax.ppermute(other, "tensor", swap)
-    own = project(rows, key_weight, value_weight, own_half, width, "own_half", after=[plan])
-    blocks = finish(plan, own, received, groups, length, "finish")
+    own_keys, own_values = (
+        times(rows, lax.dynamic_slice_in_dim(weight, own_half * width, width, 1))
+        for weight in (key_weight, value_weight)
+    )
+    blocks = finish(plan, own_keys, own_values, received, groups, length, "finish")
     arrived = {0: blocks[0]}
 
-    def send(shift, *after):
-        block = lax.optimization_barrier((blocks[shift], *after))[0]
-        arrived[shift] = lax.ppermute(block, "dp", [(g, g ^ shift) for g in range(groups)])
-
-    for shift in order[1 : IN_FLIGHT + 1]:
-        send(shift)
-    state = rubric_attention(rubric_query, rubric_key, rubric_value, blocks[0])
-    out = None
-    for at, shift in enumerate(order):
-        if at and at + IN_FLIGHT < len(order):
-            send(order[at + IN_FLIGHT], arrived[shift], state[2])
-        state, out = response_attention(shift, plan, arrived[shift], state, out)
+    def send(shifts, *after):
+        for shift in shifts:
+            block = lax.optimization_barrier((blocks[shift], *after))[0]
+            arrived[shift] = lax.ppermute(block, "dp", [(g, g ^ shift) for g in range(groups)])
+
+    send(order[:2])
+    half = pairs // 2
+    state = rubric_attention(
+        0, half, rubric_query, rubric_key, rubric_value, (), blocks[0]
+    )
+    send(order[2:4], state[2])
+    state = rubric_attention(
+        half, pairs - half, rubric_query, rubric_key, rubric_value, state, arrived[order[1]]
+    )
+    state, out = response_attention(0, plan, blocks[0], state, None)
+    for at in range(0, len(order), 2):
+        send(order[at + 4 : at + 6], arrived[order[at]], state[2])
+        for shift in order[at : at + 2]:
+            state, out = response_attention(shift, plan, arrived[shift], state, out)
     return out
 
 

time: 92.9 us -> 84.3 us (0.907)
  the two profiles are of different devices: /device:TPU:16 before, /device:TPU:0 now
where the time goes in v3:
time: 84.3 us; the launch traced here: 84.1 us
  Pallas kernels  54.6 us (65%)
  starting transfers between devices  17.9 us (21%)
  matrix products  8.79 us (10%)
  waiting for transfers between devices  1.63 us (2%)
  local copies, waits for them, and re-layouts  1.1 us (1%)
    pallas_call x8, Pallas kernels, response_attention(): pl.pallas_call(functools.partial(response_kernel, shift), grid_spec=pltpu...  32.8 us
    ppermute x7, starting transfers between devices, send(): lax.ppermute(block, 'dp', [(g, g ^ shift) for g in range(groups)])  17.4 us
    pallas_call x2, Pallas kernels, rubric_attention(): pl.pallas_call(rubric_kernel, grid=(some, steps), in_specs=[across(step_w...  11.3 us
    pallas_call x1, Pallas kernels, project_and_plan(): pl.pallas_call(functools.partial(project_rows_kernel, groups, stored), gr...  9.45 us
    dot_general x2, matrix products, times(): return jnp.dot(a, b, preferred_element_type=jnp.float32)  8.79 us
  transfers between devices with their start and end apart: 8, of which 2 were waited for; matrix products, arithmetic and copies ran while one was open for 10% of the time, Pallas kernels for 47%

profile of v3, /device:TPU:0, one launch (start us, length us, event | category | flops | bytes accessed | tf_op | source)
XLA Modules:
  0.0 84.1 jit_solution(10608308113755015409)
XLA Ops:
  0.0 9.4 %other_half.1 = (f32[1024,512]{1,0:T(8,128)}, s32[40]{0:T(128)}) custom-call(s32[1]{0:T(128)} %bitcast.half_ref, s32[1]{0:T(128)} %bitcast.1.me_ref, s32[32]{0:T(128)} %owner_ref.1, s32[32]{0:T(128)} %length_ref.1, s32[2,32]{1,0:T(2,128)} %bitcast.13, s32[8]{0:T(128)} %constant.18.clone.place_ref, bf16[1024,4096]{1,0:T(8,128)(2,1)} %bitcast.10, ...), custom_call_target="tpu_custom_call" | custom-call | flops 4294967296 | bytes 14680064 | tf_op jit(solution)/shard_map/other_half/pallas_call | solution.py:84
  9.4 0.5 collective-permute-start
  9.9 6.5 %fusion.4.own_keys_ref = f32[1024,256]{1,0:T(8,128)S(1)} fusion(bf16[1024,4096]{1,0:T(8,128)(2,1)} %bitcast.11, bf16[4096,512]{1,0:T(8,128)(2,1)} %key_ref.1, s32[]{:T(128)S(6)} %select_n.4), kind=kOutput, calls=%fused_computation.4 | convolution fusion | flops 2147483648 | bytes 11534340 | tf_op jit(solution)/shard_map/dot_general | solution.py:132
  16.4 1.1 %copy-done.5 = bf16[4096,512]{1,0:T(8,128)(2,1)S(1)} copy-done((bf16[4096,512]{1,0:T(8,128)(2,1)S(1)}, bf16[4096,512]{1,0:T(8,128)(2,1)}, u32[]{:S(2)}) %copy-start.5) | copy-done | bytes 4194328
  17.5 2.3 %fusion.7.own_values_ref = f32[1024,256]{1,0:T(8,128)S(1)} fusion(bf16[1024,4096]{1,0:T(8,128)(2,1)S(1)} %bitcast.12, bf16[4096,512]{1,0:T(8,128)(2,1)S(1)} %copy-done.5, s32[]{:T(128)S(6)} %select_n.4), kind=kOutput, calls=%fused_computation.5 | convolution fusion | flops 2147483648 | bytes 11534340 | tf_op jit(solution)/shard_map/dot_general | solution.py:132
  19.9 1.0 %finish.1 = (bf16[512,256]{1,0:T(8,128)(2,1)S(1)}, bf16[512,256]{1,0:T(8,128)(2,1)S(1)}, bf16[512,256]{1,0:T(8,128)(2,1)S(1)}, bf16[512,256]{1,0:T(8,128)(2,1)S(...) custom-call(s32[40]{0:T(128)S(1)} %copy-done.3, ...), custom_call_target="tpu_custom_call" | custom-call | flops 1048576 | bytes 6291456 | tf_op jit(solution)/shard_map/finish/pallas_call | solution.py:116
  20.9 3.6 %collective-permute-start.1 = (bf16[512,256]{1,0:T(8,128)(2,1)S(1)}, bf16[512,256]{1,0:T(8,128)(2,1)S(1)}, u32[]{:S(2)}, u32[]{:S(2)}) collective-permute-start(bf16[512,256]{1,0:T(8,128)(2,1)S(1)} %get-tuple-element.59), channel_id=1, source_target_pairs={{0,6},{2,4},{4,2},{6,0},{8,14},{10,12},{12,10},{14,8},{1,7},{3,5},... | collective-permute-start | bytes 786440 | tf_op jit(solution)/shard_map/ppermute | solution.py:354
  24.5 2.4 %collective-permute-start.3 = (bf16[512,256]{1,0:T(8,128)(2,1)S(1)}, bf16[512,256]{1,0:T(8,128)(2,1)S(1)}, u32[]{:S(2)}, u32[]{:S(2)}) collective-permute-start(bf16[512,256]{1,0:T(8,128)(2,1)S(1)} %get-tuple-element.69), channel_id=1, source_target_pairs={{0,14},{2,12},{4,10},{6,8},{8,6},{10,4},{12,2},{14,0},{1,15},{3,13... | collective-permute-start | bytes 786440 | tf_op jit(solution)/shard_map/ppermute | solution.py:354
  26.9 5.6 %rubric_attention.2 = (bf16[4,2048,256]{2,1,0:T(8,128)(2,1)S(1)}, f32[4,2048,256]{2,1,0:T(8,128)S(1)}, f32[4,16,256]{2,1,0:T(8,128)S(1)}, f32[4,16,256]{2,1,0:T(8,128)S(1)}) custom-call(bf16[4,256,2048]{2,1,0:T(8,128)(2,1)S(1)} %copy-done, bf16[4,256,256]{2,1,0:T(8,128)(2,1)S(1)} %copy-done.1, bf16[4,256,256]{2,1,0:T(8,128)(2,1)S(1)} %copy-done.2, ...), custom_call_target="tpu_custom_call" | custom-call | flops 805306368 | bytes 8388608 | tf_op jit(solution)/shard_map/rubric_attention/pallas_call | solution.py:209
  32.6 1.4 %collective-permute-start.2 = (bf16[512,256]{1,0:T(8,128)(2,1)S(1)}, bf16[512,256]{1,0:T(8,128)(2,1)S(1)}, u32[]{:S(2)}, u32[]{:S(2)}) collective-permute-start(bf16[512,256]{1,0:T(8,128)(2,1)S(1)} %get-tuple-element.68), channel_id=1, source_target_pairs={{0,12},{2,14},{4,8},{6,10},{8,4},{10,6},{12,0},{14,2},{1,13},{3,15... | collective-permute-start | bytes 786440 | tf_op jit(solution)/shard_map/ppermute | solution.py:354
  34.0 0.2 collective-permute-done.1.refs_0_.kv_ref
  34.2 5.6 %rubric_attention.3 = (bf16[4,2048,256]{2,1,0:T(8,128)(2,1)S(1)}, f32[4,2048,256]{2,1,0:T(8,128)S(1)}, f32[4,16,256]{2,1,0:T(8,128)S(1)}, f32[4,16,256]{2,1,0:T(8,128)S(1)}) custom-call(bf16[4,256,2048]{2,1,0:T(8,128)(2,1)S(1)} %copy-done, ...), custom_call_target="tpu_custom_call", output_to_operand_aliasing={{0}: (4, {}), {1}: (5, {}), {2}: (6, {}), {3}: (7, {})} | custom-call | flops 805306368 | bytes 8388608 | tf_op jit(solution)/shard_map/rubric_attention/pallas_call | solution.py:209
  39.9 3.9 %response_attention.8 = (f32[4,2048,256]{2,1,0:T(8,128)S(1)}, f32[4,16,256]{2,1,0:T(8,128)S(1)}, f32[4,16,256]{2,1,0:T(8,128)S(1)}, bf16[4,256,2048]{2,1,0:T(8,128)(2,1)}) custom-call(s32[40]{0:T(128)S(1)} %copy-done.3, bf16[4,2048,256]{2,1,0:T(8,128)(2,1)S(1)} %get-tuple-element.65.qt_ref, ...), custom_call_target="tpu_custom_call", output_to_operand_aliasing={{0}: (3, {}), {1}: (4, {}), {2}: (5, {})} | custom-call | flops 536870912 | bytes 6291456 | tf_op jit(solution)/shard_map/response_attention/pallas_call | solution.py:294
  43.7 1.3 %collective-permute-start.5 = (bf16[512,256]{1,0:T(8,128)(2,1)S(1)}, bf16[512,256]{1,0:T(8,128)(2,1)S(1)}, u32[]{:S(2)}, u32[]{:S(2)}) collective-permute-start(bf16[512,256]{1,0:T(8,128)(2,1)S(1)} %get-tuple-element.84), channel_id=1, source_target_pairs={{0,2},{2,0},{4,6},{6,4},{8,10},{10,8},{12,14},{14,12},{1,3},{3,1},... | collective-permute-start | bytes 786440 | tf_op jit(solution)/shard_map/ppermute | solution.py:354
  45.0 7.3 %collective-permute-start.6 = (bf16[512,256]{1,0:T(8,128)(2,1)S(1)}, bf16[512,256]{1,0:T(8,128)(2,1)S(1)}, u32[]{:S(2)}, u32[]{:S(2)}) collective-permute-start(bf16[512,256]{1,0:T(8,128)(2,1)S(1)} %get-tuple-element.86), channel_id=1, source_target_pairs={{0,10},{2,8},{4,14},{6,12},{8,2},{10,0},{12,6},{14,4},{1,11},{3,9}... | collective-permute-start | bytes 786440 | tf_op jit(solution)/shard_map/ppermute | solution.py:354
  52.3 3.9 %response_attention.9 = (f32[4,2048,256]{2,1,0:T(8,128)S(1)}, f32[4,16,256]{2,1,0:T(8,128)S(1)}, f32[4,16,256]{2,1,0:T(8,128)S(1)}, bf16[4,256,2048]{2,1,0:T(8,128)(2,1)}) custom-call(s32[40]{0:T(128)S(1)} %copy-done.3, bf16[4,2048,256]{2,1,0:T(8,128)(2,1)S(1)} %get-tuple-element.65.qt_ref, ...), custom_call_target="tpu_custom_call", output_to_operand_aliasing={{0}: (3, {}), {1}: (4, {}), {2}: (5, {}), {3}: (6, {})} | custom-call | flops 536870912 | bytes 6291456 | tf_op jit(solution)/shard_map/response_attention/pallas_call | solution.py:294
  56.2 4.0 %response_attention.10 = (f32[4,2048,256]{2,1,0:T(8,128)S(1)}, f32[4,16,256]{2,1,0:T(8,128)S(1)}, f32[4,16,256]{2,1,0:T(8,128)S(1)}, bf16[4,256,2048]{2,1,0:T(8,128)(2,1)}) custom-call(s32[40]{0:T(128)S(1)} %copy-done.3, bf16[4,2048,256]{2,1,0:T(8,128)(2,1)S(1)} %get-tuple-element.65.qt_ref, ...), custom_call_target="tpu_custom_call", output_to_operand_aliasing={{0}: (3, {}), {1}: (4, {}), {2}: (5, {}), {3}: (6, {})} | custom-call | flops 536870912 | bytes 6291456 | tf_op jit(solution)/shard_map/response_attention/pallas_call | solution.py:294
  60.2 1.4 %collective-permute-start.4 = (bf16[512,256]{1,0:T(8,128)(2,1)S(1)}, bf16[512,256]{1,0:T(8,128)(2,1)S(1)}, u32[]{:S(2)}, u32[]{:S(2)}) collective-permute-start(bf16[512,256]{1,0:T(8,128)(2,1)S(1)} %get-tuple-element.82), channel_id=1, source_target_pairs={{0,8},{2,10},{4,12},{6,14},{8,0},{10,2},{12,4},{14,6},{1,9},{3,11}... | collective-permute-start | bytes 786440 | tf_op jit(solution)/shard_map/ppermute | solution.py:354
  61.6 3.9 %response_attention.11 = (f32[4,2048,256]{2,1,0:T(8,128)S(1)}, f32[4,16,256]{2,1,0:T(8,128)S(1)}, f32[4,16,256]{2,1,0:T(8,128)S(1)}, bf16[4,256,2048]{2,1,0:T(8,128)(2,1)}) custom-call(s32[40]{0:T(128)S(1)} %copy-done.3, bf16[4,2048,256]{2,1,0:T(8,128)(2,1)S(1)} %get-tuple-element.65.qt_ref, ...), custom_call_target="tpu_custom_call", output_to_operand_aliasing={{0}: (3, {}), {1}: (4, {}), {2}: (5, {}), {3}: (6, {})} | custom-call | flops 536870912 | bytes 6291456 | tf_op jit(solution)/shard_map/response_attention/pallas_call | solution.py:294
  65.5 4.3 %response_attention.12 = (f32[4,2048,256]{2,1,0:T(8,128)S(1)}, f32[4,16,256]{2,1,0:T(8,128)S(1)}, f32[4,16,256]{2,1,0:T(8,128)S(1)}, bf16[4,256,2048]{2,1,0:T(8,128)(2,1)}) custom-call(s32[40]{0:T(128)S(1)} %copy-done.3, bf16[4,2048,256]{2,1,0:T(8,128)(2,1)S(1)} %get-tuple-element.65.qt_ref, ...), custom_call_target="tpu_custom_call", output_to_operand_aliasing={{0}: (3, {}), {1}: (4, {}), {2}: (5, {}), {3}: (6, {})} | custom-call | flops 536870912 | bytes 6291456 | tf_op jit(solution)/shard_map/response_attention/pallas_call | solution.py:294
  69.8 1.4 %collective-permute-done.6.kv_ref = bf16[512,256]{1,0:T(8,128)(2,1)S(1)} collective-permute-done((bf16[512,256]{1,0:T(8,128)(2,1)S(1)}, bf16[512,256]{1,0:T(8,128)(2,1)S(1)}, u32[]{:S(2)}, u32[]{:S(2)}) %collective-permute-start.6) | collective-permute-done | bytes 262176 | tf_op jit(solution)/shard_map/ppermute | solution.py:354
  71.2 4.3 %response_attention.13 = (f32[4,2048,256]{2,1,0:T(8,128)S(1)}, f32[4,16,256]{2,1,0:T(8,128)S(1)}, f32[4,16,256]{2,1,0:T(8,128)S(1)}, bf16[4,256,2048]{2,1,0:T(8,128)(2,1)}) custom-call(s32[40]{0:T(128)S(1)} %copy-done.3, bf16[4,2048,256]{2,1,0:T(8,128)(2,1)S(1)} %get-tuple-element.65.qt_ref, ...), custom_call_target="tpu_custom_call", output_to_operand_aliasing={{0}: (3, {}), {1}: (4, {}), {2}: (5, {}), {3}: (6, {})} | custom-call | flops 536870912 | bytes 6291456 | tf_op jit(solution)/shard_map/response_attention/pallas_call | solution.py:294
  75.5 4.3 %response_attention.14 = (f32[4,2048,256]{2,1,0:T(8,128)S(1)}, f32[4,16,256]{2,1,0:T(8,128)S(1)}, f32[4,16,256]{2,1,0:T(8,128)S(1)}, bf16[4,256,2048]{2,1,0:T(8,128)(2,1)}) custom-call(s32[40]{0:T(128)S(1)} %copy-done.3, bf16[4,2048,256]{2,1,0:T(8,128)(2,1)S(1)} %get-tuple-element.65.qt_ref, ...), custom_call_target="tpu_custom_call", output_to_operand_aliasing={{0}: (3, {}), {1}: (4, {}), {2}: (5, {}), {3}: (6, {})} | custom-call | flops 536870912 | bytes 6291456 | tf_op jit(solution)/shard_map/response_attention/pallas_call | solution.py:294
  79.8 4.3 %response_attention.15 = (f32[4,2048,256]{2,1,0:T(8,128)S(1)}, f32[4,16,256]{2,1,0:T(8,128)S(1)}, f32[4,16,256]{2,1,0:T(8,128)S(1)}, bf16[4,256,2048]{2,1,0:T(8,128)(2,1)}) custom-call(s32[40]{0:T(128)S(1)} %copy-done.3, bf16[4,2048,256]{2,1,0:T(8,128)(2,1)S(1)} %get-tuple-element.65.qt_ref, ...), custom_call_target="tpu_custom_call", output_to_operand_aliasing={{0}: (3, {}), {1}: (4, {}), {2}: (5, {}), {3}: (6, {})} | custom-call | flops 536870912 | bytes 6291456 | tf_op jit(solution)/shard_map/response_attention/pallas_call | solution.py:294
  (18 shorter events, 0.0 us)
Async XLA Ops:
  9.4 10.4 %collective-permute-start = (f32[1024,512]{1,0:T(8,128)}, f32[1024,512]{1,0:T(8,128)S(1)}, u32[]{:S(2)}, u32[]{:S(2)}) collective-permute-start(f32[1024,512]{1,0:T(8,128)} %get-tuple-element.58), channel_id=1, source_target_pairs={{0,1},{1,0},{2,3},{3,2},{4,5},{5,4},{6,7},{7,6},{8,9},{9,8},{10,11... | collective-permute-start | bytes 6291464 | tf_op jit(solution)/shard_map/ppermute | solution.py:343
  9.9 6.5 %copy-start.4 = (bf16[4,256,4096]{2,1,0:T(8,128)(2,1)S(1)}, bf16[4,256,4096]{2,1,0:T(8,128)(2,1)}, u32[]{:S(2)}) copy-start(bf16[4,256,4096]{2,1,0:T(8,128)(2,1)} %param.13) | copy-start | bytes 25165828
  9.9 7.6 %copy-start.5 = (bf16[4096,512]{1,0:T(8,128)(2,1)S(1)}, bf16[4096,512]{1,0:T(8,128)(2,1)}, u32[]{:S(2)}) copy-start(bf16[4096,512]{1,0:T(8,128)(2,1)} %value_ref.1) | copy-start | bytes 12582916
  17.5 2.4 %copy-start.3 = (s32[40]{0:T(128)S(1)}, s32[40]{0:T(128)}, u32[]{:S(2)}) copy-start(s32[40]{0:T(128)} %get-tuple-element.57.plan_ref) | copy-start | bytes 484
  17.5 9.4 %copy-start.1 = (bf16[4,256,256]{2,1,0:T(8,128)(2,1)S(1)}, bf16[4,256,256]{2,1,0:T(8,128)(2,1)}, u32[]{:S(2)}) copy-start(bf16[4,256,256]{2,1,0:T(8,128)(2,1)} %k_ref.3) | copy-start | bytes 1572868
  17.5 9.4 %copy-start.2 = (bf16[4,256,256]{2,1,0:T(8,128)(2,1)S(1)}, bf16[4,256,256]{2,1,0:T(8,128)(2,1)}, u32[]{:S(2)}) copy-start(bf16[4,256,256]{2,1,0:T(8,128)(2,1)} %v_ref.3) | copy-start | bytes 1572868
  19.8 7.1 %copy-start = (bf16[4,256,2048]{2,1,0:T(8,128)(2,1)S(1)}, bf16[4,256,2048]{2,1,0:T(8,128)(2,1)}, u32[]{:S(2)}) copy-start(bf16[4,256,2048]{2,1,0:T(8,128)(2,1)} %q_ref.3) | copy-start | bytes 12582916
  20.9 13.3 %collective-permute-start.1 = (bf16[512,256]{1,0:T(8,128)(2,1)S(1)}, bf16[512,256]{1,0:T(8,128)(2,1)S(1)}, u32[]{:S(2)}, u32[]{:S(2)}) collective-permute-start(bf16[512,256]{1,0:T(8,128)(2,1)S(1)} %get-tuple-element.59), channel_id=1, source_target_pairs={{0,6},{2,4},{4,2},{6,0},{8,14},{10,12},{12,10},{14,8},{1,7},{3,5},... | collective-permute-start | bytes 786440 | tf_op jit(solution)/shard_map/ppermute | solution.py:354
  24.5 19.2 %collective-permute-start.3 = (bf16[512,256]{1,0:T(8,128)(2,1)S(1)}, bf16[512,256]{1,0:T(8,128)(2,1)S(1)}, u32[]{:S(2)}, u32[]{:S(2)}) collective-permute-start(bf16[512,256]{1,0:T(8,128)(2,1)S(1)} %get-tuple-element.69), channel_id=1, source_target_pairs={{0,14},{2,12},{4,10},{6,8},{8,6},{10,4},{12,2},{14,0},{1,15},{3,13... | collective-permute-start | bytes 786440 | tf_op jit(solution)/shard_map/ppermute | solution.py:354
  32.6 27.7 %collective-permute-start.2 = (bf16[512,256]{1,0:T(8,128)(2,1)S(1)}, bf16[512,256]{1,0:T(8,128)(2,1)S(1)}, u32[]{:S(2)}, u32[]{:S(2)}) collective-permute-start(bf16[512,256]{1,0:T(8,128)(2,1)S(1)} %get-tuple-element.68), channel_id=1, source_target_pairs={{0,12},{2,14},{4,8},{6,10},{8,4},{10,6},{12,0},{14,2},{1,13},{3,15... | collective-permute-start | bytes 786440 | tf_op jit(solution)/shard_map/ppermute | solution.py:354
  34.0 31.5 %collective-permute-start.7 = (bf16[512,256]{1,0:T(8,128)(2,1)S(1)}, bf16[512,256]{1,0:T(8,128)(2,1)S(1)}, u32[]{:S(2)}, u32[]{:S(2)}) collective-permute-start(bf16[512,256]{1,0:T(8,128)(2,1)S(1)} %get-tuple-element.88), channel_id=1, source_target_pairs={{0,4},{2,6},{4,0},{6,2},{8,12},{10,14},{12,8},{14,10},{1,5},{3,7},... | collective-permute-start | bytes 786440 | tf_op jit(solution)/shard_map/ppermute | solution.py:354
  43.7 31.7 %collective-permute-start.5 = (bf16[512,256]{1,0:T(8,128)(2,1)S(1)}, bf16[512,256]{1,0:T(8,128)(2,1)S(1)}, u32[]{:S(2)}, u32[]{:S(2)}) collective-permute-start(bf16[512,256]{1,0:T(8,128)(2,1)S(1)} %get-tuple-element.84), channel_id=1, source_target_pairs={{0,2},{2,0},{4,6},{6,4},{8,10},{10,8},{12,14},{14,12},{1,3},{3,1},... | collective-permute-start | bytes 786440 | tf_op jit(solution)/shard_map/ppermute | solution.py:354
  45.0 26.2 %collective-permute-start.6 = (bf16[512,256]{1,0:T(8,128)(2,1)S(1)}, bf16[512,256]{1,0:T(8,128)(2,1)S(1)}, u32[]{:S(2)}, u32[]{:S(2)}) collective-permute-start(bf16[512,256]{1,0:T(8,128)(2,1)S(1)} %get-tuple-element.86), channel_id=1, source_target_pairs={{0,10},{2,8},{4,14},{6,12},{8,2},{10,0},{12,6},{14,4},{1,11},{3,9}... | collective-permute-start | bytes 786440 | tf_op jit(solution)/shard_map/ppermute | solution.py:354
  60.2 19.5 %collective-permute-start.4 = (bf16[512,256]{1,0:T(8,128)(2,1)S(1)}, bf16[512,256]{1,0:T(8,128)(2,1)S(1)}, u32[]{:S(2)}, u32[]{:S(2)}) collective-permute-start(bf16[512,256]{1,0:T(8,128)(2,1)S(1)} %get-tuple-element.82), channel_id=1, source_target_pairs={{0,8},{2,10},{4,12},{6,14},{8,0},{10,2},{12,4},{14,6},{1,9},{3,11}... | collective-permute-start | bytes 786440 | tf_op jit(solution)/shard_map/ppermute | solution.py:354
